TPU v7x, 256 devices: a whole 4x4x8 slice. The times are simulated.
256 devices in a mesh: clip: 4 (over y_lo, core), tm: 32 (over x, z), mp: 2 (over y_hi).
Axes of the slice: x: 4, y: 4 (y_hi: 2, y_lo: 2; y = y_hi * 2 + y_lo), z: 8, core: 2. Of those that a mesh axis runs over, the one named last changes fastest.
Arguments:
- video: bfloat16 [128, 576, 1024], P(('clip', 'tm')), parts along dimension 0, may hold values from -6 to 6
- gain_time: float32 [1024], replicated, may hold values from 0.1 to 1.9
- qkv_time: bfloat16 [1024, 3, 1024], P(None, None, 'mp'), may hold values from -2 to 2
- proj_time: bfloat16 [1024, 1024], P('mp'), may hold values from -0.1875 to 0.1875
- gain_space: float32 [1024], replicated, may hold values from 0.1 to 1.9
- qkv_space: bfloat16 [1024, 3, 1024], P(None, None, 'mp'), may hold values from -2 to 2
- proj_space: bfloat16 [1024, 1024], P('mp'), may hold values from -0.1875 to 0.1875
Outputs:
- encoded: bfloat16 [128, 576, 1024], P(('clip', 'tm')), parts along dimension 0
There are 4 independent parts, one for each index of `clip`. A program takes and returns all parts, laid end to end along the dimension named above; an argument that names none is the same for every part. Nothing has to cross between parts.
All inputs are finite; a program needn't handle non-finite values.
Results may differ from a plain program's by a relative error of at most 0.04.
Values may be sent and summed in bfloat16 or wider, within the bound.
No kernel may reach another device: no remote copies, remote signals or barrier semaphores. Data moves between devices by JAX's collectives and lax.ppermute only.
A program may use at most 128 MiB of HBM per device.

v0:
```python
import jax
import jax.numpy as jnp
from jax import lax
from jax.sharding import PartitionSpec as P

HD = 64


def layer_norm(values, gain):
    wide = values.astype(jnp.float32)
    center = jnp.mean(wide, axis=-1, keepdims=True)
    spread = jnp.mean((wide - center) ** 2, axis=-1, keepdims=True)
    return ((wide - center) * lax.rsqrt(spread + 1e-05) * gain).astype(jnp.bfloat16)


def project(normed, weights):
    width = normed.shape[-1]
    local = weights.shape[-1]
    lead = normed.shape[:-1]
    flat = jnp.dot(
        normed.reshape(-1, width),
        weights.reshape(width, 3 * local),
        preferred_element_type=jnp.float32,
    )
    return flat.astype(jnp.bfloat16).reshape(lead + (3, local))


def temporal_heads(query, keys, values):
    frames, patches, local = (query.shape[0], query.shape[1], query.shape[-1])
    shaped = (frames, patches, local // HD, HD)
    scale = 1.0 / jnp.sqrt(jnp.float32(HD))
    scores = (
        jnp.einsum(
            "fphd,gphd->phfg",
            query.reshape(shaped),
            keys.reshape(shaped),
            preferred_element_type=jnp.float32,
        )
        * scale
    )
    weights = jax.nn.softmax(scores, axis=-1).astype(jnp.bfloat16)
    result = jnp.einsum(
        "phfg,gphd->fphd", weights, values.reshape(shaped), preferred_element_type=jnp.float32
    )
    return result.astype(jnp.bfloat16).reshape(query.shape)


def spatial_frame(triple):
    q_one, k_one, v_one = triple
    patches, local = q_one.shape
    shaped = (patches, local // HD, HD)
    scale = 1.0 / jnp.sqrt(jnp.float32(HD))
    scores = (
        jnp.einsum(
            "phd,qhd->hpq",
            q_one.reshape(shaped),
            k_one.reshape(shaped),
            preferred_element_type=jnp.float32,
        )
        * scale
    )
    weights = jax.nn.softmax(scores, axis=-1).astype(jnp.bfloat16)
    result = jnp.einsum(
        "hpq,qhd->phd", weights, v_one.reshape(shaped), preferred_element_type=jnp.float32
    )
    return result.astype(jnp.bfloat16).reshape(patches, local)


def temporal_items(triple):
    query, keys, values = triple
    lead = query.shape[:2]
    joined = temporal_heads(
        query.reshape(lead + (-1,)), keys.reshape(lead + (-1,)), values.reshape(lead + (-1,))
    )
    joined = joined.reshape(query.shape)
    return lax.all_to_all(joined, "tm", split_axis=0, concat_axis=1, tiled=True)


def shards(video, gain_time, qkv_time, proj_time, gain_space, qkv_space, proj_space):
    frames, patches, width = video.shape
    local = qkv_time.shape[-1]
    pairs = local // (2 * HD)
    normed = layer_norm(video, gain_time)
    triple = project(normed, qkv_time).reshape(frames, patches, 3, pairs, 2 * HD)
    attended = temporal_items(
        (
            lax.all_to_all(triple[:, :, 0], "tm", split_axis=1, concat_axis=0, tiled=True),
            lax.all_to_all(triple[:, :, 1], "tm", split_axis=1, concat_axis=0, tiled=True),
            lax.all_to_all(triple[:, :, 2], "tm", split_axis=1, concat_axis=0, tiled=True),
        )
    )
    partial_sum = jnp.dot(
        attended.reshape(frames * patches, local), proj_time, preferred_element_type=jnp.float32
    )
    summed = lax.psum(partial_sum.astype(jnp.bfloat16), "mp").astype(jnp.float32)
    middle = (video.astype(jnp.float32) + summed.reshape(video.shape)).astype(jnp.bfloat16)
    triple = project(layer_norm(middle, gain_space), qkv_space)
    attended = lax.map(spatial_frame, (triple[:, :, 0], triple[:, :, 1], triple[:, :, 2]))
    partial_sum = jnp.dot(
        attended.reshape(frames * patches, local), proj_space, preferred_element_type=jnp.float32
    )
    summed = lax.psum(partial_sum.astype(jnp.bfloat16), "mp").astype(jnp.float32)
    return (middle.astype(jnp.float32) + summed.reshape(video.shape)).astype(jnp.bfloat16)


def solution(mesh):
    placed = (
        P(("clip", "tm"), None, None),
        P(),
        P(None, None, "mp"),
        P("mp", None),
        P(),
        P(None, None, "mp"),
        P("mp", None),
    )
    return jax.shard_map(
        shards, mesh=mesh, in_specs=placed, out_specs=P(("clip", "tm"), None, None), check_vma=False
    )
```

profile of v0, /device:TPU:1, one launch (start us, length us, event | category | flops | bytes accessed | tf_op | source)
XLA Modules:
  0.0 282.0 jit_solution(2222894533416601169)
XLA Ops:
  6.5 1.6 convert_reduce_fusion.1
  8.1 1.7 fusion.14
  9.9 4.8 %copy.25 = bf16[1024,3,512]{0,2,1:T(8,128)(2,1)} copy(bf16[1024,3,512]{2,0,1:T(8,128)(2,1)} %param.9) | data formatting | bytes 6291456 | tf_op args[2]
  14.7 5.2 %convolution_convert_fusion.1 = bf16[576,1536]{1,0:T(8,128)(2,1)} fusion(bf16[1024,1536]{0,1:T(8,128)(2,1)} %bitcast.58, bf16[1,576,1024]{2,1,0:T(8,128)(2,1)S(1)} %copy-done.1, f32[1024]{0:T(1024)S(1)} %copy-done.4, f32[576]{0:T(1024)S(1)} %add_rsqrt_fusion.1, f32[576]{0:T(1024)S(1)} %broadcast_multiply_fusion.1), kind=kOutput, calls=%fused_computation.15 | convolution fusion | flops 1815773184 | bytes 6103552 | tf_op jit(solution)/shard_map/dot_general | solution.py:20
  19.9 4.1 %reshape_reshape.15 = bf16[1,576,3,4,128]{4,3,2,1,0:T(4,128)(2,1)} reshape(bf16[576,1536]{1,0:T(8,128)(2,1)} %convolution_convert_fusion.1) | data formatting | bytes 3538944 | tf_op jit(solution)/shard_map/reshape;reshape | solution.py:84
  24.0 2.9 %slice_bitcast_fusion.2 = (bf16[1,576,4,128]{3,2,0,1:T(4,128)(2,1)}, bf16[1,576,4,128]{3,2,0,1:T(4,128)(2,1)S(1)}, bf16[1,576,4,128]{3,2,0,1:T(4,128)(2,1)S(1)}) fusion(bf16[1,576,3,4,128]{4,3,2,1,0:T(4,128)(2,1)} %reshape_reshape.15), kind=kLoop, calls=%fused_computation.58 | loop fusion | bytes 3538944 | tf_op jit(solution)/shard_map/squeeze | solution.py:89
  26.9 27.0 %all_to_all.16 = bf16[1,576,4,128]{3,2,0,1:T(4,128)(2,1)} all-to-all(bf16[1,576,4,128]{3,2,0,1:T(4,128)(2,1)S(1)} %get-tuple-element.26), channel_id=1, replica_groups=mesh['clip'=4,'tm'=32,'mp'=2] {'tm'}, dimensions={1} | all-to-all | bytes 1179648 | tf_op jit(solution)/shard_map/all_to_all | solution.py:87
  53.9 22.8 %all_to_all.17 = bf16[1,576,4,128]{3,2,0,1:T(4,128)(2,1)} all-to-all(bf16[1,576,4,128]{3,2,0,1:T(4,128)(2,1)S(1)} %get-tuple-element.27), channel_id=1, replica_groups=mesh['clip'=4,'tm'=32,'mp'=2] {'tm'}, dimensions={1} | all-to-all | bytes 1179648 | tf_op jit(solution)/shard_map/all_to_all | solution.py:88
  76.7 8.0 %all-to-all-start = ((bf16[1,576,4,128]{3,2,0,1:T(4,128)(2,1)}), bf16[1,576,4,128]{3,2,0,1:T(4,128)(2,1)}, u32[]{:S(2)}, u32[]{:S(2)}) async-start(bf16[1,576,4,128]{3,2,0,1:T(4,128)(2,1)} %get-tuple-element.25), calls=%async_computation | async-start | bytes 1179648 | tf_op jit(solution)/shard_map/all_to_all | solution.py:89
  84.8 1.8 reshape_reshape.18
  86.6 2.6 reshape_reshape.17
  89.2 2.0 fusion.33
  91.2 2.1 fusion.50
  93.4 6.1 %all-to-all-done = bf16[1,576,4,128]{3,2,0,1:T(4,128)(2,1)} async-done(((bf16[1,576,4,128]{3,2,0,1:T(4,128)(2,1)}), bf16[1,576,4,128]{3,2,0,1:T(4,128)(2,1)}, u32[]{:S(2)}, u32[]{:S(2)}) %all-to-all-start) | async-done | bytes 589856 | tf_op jit(solution)/shard_map/all_to_all | solution.py:89
  99.4 1.8 reshape_reshape.16
  101.2 2.3 fusion.24
  103.6 0.5 copy.33
  104.0 1.4 reshape_reshape.19
  105.4 22.7 %all_to_all.18 = bf16[32,18,4,128]{3,2,1,0:T(4,128)(2,1)S(1)} all-to-all(bf16[32,18,4,128]{3,2,1,0:T(4,128)(2,1)} %reshape_reshape.19), channel_id=1, replica_groups=mesh['clip'=4,'tm'=32,'mp'=2] {'tm'}, dimensions={0} | all-to-all | bytes 1179648 | tf_op jit(solution)/shard_map/all_to_all | solution.py:76
  128.2 1.8 fusion.22
  130.0 4.7 %copy.34 = bf16[1024,3,512]{0,2,1:T(8,128)(2,1)} copy(bf16[1024,3,512]{2,0,1:T(8,128)(2,1)} %param.12) | data formatting | bytes 6291456 | tf_op args[5]
  134.7 52.9 %all-reduce.3.cloned.1.call-done = bf16[1,576,1024]{2,1,0:T(8,128)(2,1)} async-done(((bf16[1,576,1024]{2,1,0:T(8,128)(2,1)}), bf16[1,576,1024]{2,1,0:T(8,128)(2,1)}) %all-reduce.3.cloned.1.call-update) | async-done | bytes 1179664 | tf_op jit(solution)/shard_map/psum | solution.py:95
  187.6 1.8 convert_reduce_fusion
  189.4 0.5 fusion.11
  189.9 3.3 %convolution_convert_fusion = bf16[576,1536]{1,0:T(8,128)(2,1)} fusion(bf16[1024,1536]{0,1:T(8,128)(2,1)S(1)} %bitcast.57, bf16[1,576,1024]{2,1,0:T(8,128)(2,1)S(1)} %get-tuple-element.14, f32[1024]{0:T(1024)S(1)} %copy-done.5, f32[576]{0:T(1024)S(1)} %add_rsqrt_fusion, f32[576]{0:T(1024)S(1)} %broadcast_multiply_fusion), kind=kOutput, calls=%fused_computation.14 | convolution fusion | flops 1815773184 | bytes 6103552 | tf_op jit(solution)/shard_map/dot_general | solution.py:20
  193.3 3.9 %copy.35 = bf16[576,1536]{0,1:T(8,128)(2,1)} copy(bf16[576,1536]{1,0:T(8,128)(2,1)} %convolution_convert_fusion) | data formatting | bytes 3538944 | tf_op jit(solution)/shard_map/convert_element_type | solution.py:25
  197.2 2.7 fusion.49
  199.9 9.4 %fusion.51 = (f32[8,576]{1,0:T(8,128)S(1)}, f32[8,576,576]{1,2,0:T(8,128)}) fusion(bf16[576,8,64]{0,2,1:T(8,128)(2,1)} %bitcast.61, bf16[576,8,64]{0,2,1:T(8,128)(2,1)} %bitcast.60), kind=kOutput, calls=%fused_computation.67 | convolution fusion | flops 347701824 | bytes 11814912 | tf_op jit(solution)/shard_map/while/body/eval_jaxpr/sub | solution.py:62
  209.3 5.6 %fusion.27 = bf16[8,64,576]{2,1,0:T(8,128)(2,1)S(1)} fusion(bf16[576,8,64]{0,2,1:T(8,128)(2,1)S(1)} %bitcast.59, f32[8,576,576]{1,2,0:T(8,128)} %get-tuple-element.31, f32[8,576]{1,0:T(8,128)S(1)} %get-tuple-element.30), kind=kOutput, calls=%fused_computation.39 | convolution fusion | flops 345341952 | bytes 11814912 | tf_op jit(solution)/shard_map/while/body/eval_jaxpr/hpq,qhd->phd/dot_general | solution.py:63
  214.9 1.8 fusion.23
  216.7 55.7 %all-reduce.5.cloned.1.call-done = bf16[1,576,1024]{2,1,0:T(8,128)(2,1)} async-done(((bf16[1,576,1024]{2,1,0:T(8,128)(2,1)}), bf16[1,576,1024]{2,1,0:T(8,128)(2,1)}) %all-reduce.5.cloned.1.call-update) | async-done | bytes 1179664 | tf_op jit(solution)/shard_map/psum | solution.py:102
  272.4 2.7 fusion.18
  (20 shorter events, 0.2 us)
Async XLA Ops:
  6.5 121.6 %copy-start = (bf16[512,1024]{1,0:T(8,128)(2,1)S(1)}, bf16[512,1024]{1,0:T(8,128)(2,1)}, u32[]{:S(2)}) copy-start(bf16[512,1024]{1,0:T(8,128)(2,1)} %param.10) | copy-start | bytes 3145732
  9.9 4.8 %copy-start.1 = (bf16[1,576,1024]{2,1,0:T(8,128)(2,1)S(1)}, bf16[1,576,1024]{2,1,0:T(8,128)(2,1)}, u32[]{:S(2)}) copy-start(bf16[1,576,1024]{2,1,0:T(8,128)(2,1)} %param.7) | copy-start | bytes 3538948
  9.9 4.8 %copy-start.4 = (f32[1024]{0:T(1024)S(1)}, f32[1024]{0:T(1024)}, u32[]{:S(2)}) copy-start(f32[1024]{0:T(1024)} %param.8) | copy-start | bytes 12292
  76.7 22.7 %all-to-all-start = ((bf16[1,576,4,128]{3,2,0,1:T(4,128)(2,1)}), bf16[1,576,4,128]{3,2,0,1:T(4,128)(2,1)}, u32[]{:S(2)}, u32[]{:S(2)}) async-start(bf16[1,576,4,128]{3,2,0,1:T(4,128)(2,1)} %get-tuple-element.25), calls=%async_computation | async-start | bytes 1179648 | tf_op jit(solution)/shard_map/all_to_all | solution.py:89
  84.8 102.8 %all-reduce.3.cloned.1.call-start = ((), (), s32[]{:S(2)}) async-start(), calls=%async_computation.4 | async-start | bytes 2359296 | tf_op jit(solution)/shard_map/psum | solution.py:95
  130.0 142.5 %all-reduce.5.cloned.1.call-start = ((), (), s32[]{:S(2)}) async-start(), calls=%async_computation.5 | async-start | bytes 2359296 | tf_op jit(solution)/shard_map/psum | solution.py:102
  134.7 55.2 %copy-start.5 = (f32[1024]{0:T(1024)S(1)}, f32[1024]{0:T(1024)}, u32[]{:S(2)}) copy-start(f32[1024]{0:T(1024)} %param.11) | copy-start | bytes 12292
  187.6 2.3 copy-start.2
  209.2 5.6 %copy-start.3 = (bf16[512,1024]{1,0:T(8,128)(2,1)S(1)}, bf16[512,1024]{1,0:T(8,128)(2,1)}, u32[]{:S(2)}) copy-start(bf16[512,1024]{1,0:T(8,128)(2,1)} %param.13) | copy-start | bytes 3145732
Sparse Core Ops, SparseCore 0:
  130.1 57.4 all-reduce.2
  216.9 55.5 all-reduce.4
where the time goes:
time: 283 us; the launch traced here: 282 us
  waiting for transfers between devices  115 us (41%)
  blocking collectives  72.6 us (26%)
  matrix products  31.5 us (11%)
  local copies, waits for them, and re-layouts  31.1 us (11%)
  between operations  13.5 us (5%)
  other arithmetic  10.5 us (4%)
  starting transfers between devices  8.12 us (3%)
    psum x2, waiting for transfers between devices, shards(): lax.psum(partial_sum.astype(jnp.bfloat16), 'mp').astype(jnp.float32)  109 us
    all_to_all x1, blocking collectives, shards(): lax.all_to_all(triple[:, :, 0], 'tm', split_axis=1, concat_axis=0, tiled=...  27 us
    all_to_all x1, blocking collectives, shards(): lax.all_to_all(triple[:, :, 1], 'tm', split_axis=1, concat_axis=0, tiled=...  22.8 us
    all_to_all x1, blocking collectives, temporal_items(): return lax.all_to_all(joined, 'tm', split_axis=0, concat_axis=1, tiled=True)  22.7 us
    unnamed x14, local copies, waits for them, and re-layouts  9.49 us
    sub x1, matrix products, spatial_frame(): weights = jax.nn.softmax(scores, axis=-1).astype(jnp.bfloat16)  9.37 us
    dot_general x2, matrix products, project(): jnp.dot(normed.reshape(-1, width), weights.reshape(width, 3 * local), pre...  8.56 us
    all_to_all x1, starting transfers between devices, shards(): lax.all_to_all(triple[:, :, 2], 'tm', split_axis=1, concat_axis=0, tiled=...  8.04 us
  transfers between devices with their start and end apart: 3, of which 3 were waited for; matrix products, arithmetic and copies ran while one was open for 5% of the time, Pallas kernels for 0%

commit v1 on v0

v1 whole, which is shorter than its diff:
```python
import functools
import math

import jax
import jax.numpy as jnp
from jax import lax
from jax.experimental import pallas as pl
from jax.experimental.pallas import tpu as pltpu
from jax.sharding import PartitionSpec as P

HD = 64
LANES = 128
ROWS = 8
F32 = jnp.float32
BF16 = jnp.bfloat16
SCALE = math.log2(math.e) / math.sqrt(HD)
EPS = 1e-05
MASKED = -1e30


def dot(left, right):
    return jnp.dot(left, right, preferred_element_type=F32)


def dot_t(left, right):
    return lax.dot_general(left, right, (((1,), (1,)), ((), ())), preferred_element_type=F32)


def iota(shape, dim):
    return lax.broadcasted_iota(jnp.int32, shape, dim)


def layer_norm(wide, gain):
    center = jnp.mean(wide, axis=-1, keepdims=True)
    moved = wide - center
    spread = jnp.mean(moved * moved, axis=-1, keepdims=True)
    return (moved * lax.rsqrt(spread + EPS) * gain).astype(BF16)


def spread_rows(rows):
    n, width = rows.shape
    groups = width // LANES
    at = iota((n * groups, n), 0)
    row = iota((n * groups, n), 1)
    total = jnp.zeros((n * groups, LANES), F32)
    for group in range(groups):
        pick = jnp.where(at == row * groups + group, 1.0, 0.0).astype(BF16)
        total = total + dot(pick, rows[:, group * LANES : (group + 1) * LANES])
    return total


def gather_rows(spread, groups):
    n = spread.shape[0] // groups
    row = iota((n, n * groups), 0)
    at = iota((n, n * groups), 1)
    parts = []
    for group in range(groups):
        pick = jnp.where(at == row * groups + group, 1.0, 0.0).astype(BF16)
        parts.append(dot(pick, spread).astype(BF16))
    return jnp.concatenate(parts, axis=1)


def store_packed(out_ref, main, extra):
    n, rows, _ = out_ref.shape
    width = main.shape[1]
    out_ref[:, :, :width] = main.reshape(n, rows, width).astype(BF16)
    out_ref[:, :, width:] = spread_rows(extra).reshape(n, rows, LANES).astype(BF16)


def load_packed(ref):
    n, rows, full = ref.shape
    width = full - LANES
    main = ref[:, :, :width].astype(F32).reshape(n * rows, width).astype(BF16)
    tail = ref[:, :, width:].astype(F32).reshape(n * rows, LANES).astype(BF16)
    return main, gather_rows(tail, rows)


def half_rows(count, mine):
    member = lax.axis_index("mp")
    place = member if mine else 1 - member
    return pl.ds(pl.multiple_of(place * count, 32), count)


def norm_kernel(x_ref, gain_ref, out_ref):
    half = x_ref.shape[0] // 2
    frames = out_ref.shape[0]
    x = x_ref[half_rows(half, True), :].astype(F32)
    normed = layer_norm(x, gain_ref[...])
    main = frames * ROWS
    store_packed(out_ref, normed[:main].astype(F32), normed[main:])


def place_pieces(pieces, target):
    clip = lax.axis_index("clip")
    count = len(pieces) // 4
    rows = target.shape[-2] // len(pieces)
    for distance in range(4):
        quarter = clip ^ distance
        for chunk in range(count):
            start = pl.multiple_of((quarter * count + chunk) * rows, rows)
            piece = pieces[distance * count + chunk]
            if len(target.shape) == 3:
                target[:, pl.ds(start, rows), :] = piece[...]
            else:
                target[pl.ds(start, rows), :] = piece[...]


def temporal_pairs(q, k, v, out, at, frames):
    rows = q.shape[0]
    block = 4 * frames
    low = iota((block, LANES), 1) < HD
    for pair in range(q.shape[1] // LANES):
        lanes = slice(pair * LANES, (pair + 1) * LANES)
        for start in range(0, rows, block):
            count = min(block, rows - start)
            key_at = start + count - block
            keys = k[key_at : key_at + block, lanes]
            vals = v[key_at : key_at + block, lanes]
            zero = jnp.zeros_like(keys)
            keys2 = jnp.concatenate([jnp.where(low, keys, zero), jnp.where(low, zero, keys)], axis=0)
            vals2 = jnp.concatenate([jnp.where(low, vals, zero), jnp.where(low, zero, vals)], axis=0)
            scores = dot_t(q[start : start + count, lanes], keys2)
            own = (iota((count, 2 * block), 0) + (start - key_at)) // frames
            other = (iota((count, 2 * block), 1) % block) // frames
            scores = jnp.where(own == other, scores, MASKED)
            first = scores[:, :block]
            second = scores[:, block:]
            e_first = jnp.exp2(first - jnp.max(first, axis=-1, keepdims=True))
            e_second = jnp.exp2(second - jnp.max(second, axis=-1, keepdims=True))
            weights = jnp.concatenate([e_first, e_second], axis=1).astype(BF16)
            r_first = 1.0 / jnp.sum(e_first, axis=-1, keepdims=True)
            r_second = 1.0 / jnp.sum(e_second, axis=-1, keepdims=True)
            result = dot(weights, vals2) * jnp.where(low[:count], r_first, r_second)
            out[start : start + count, at + pair * LANES : at + (pair + 1) * LANES] = result.astype(BF16)


def temporal_kernel(count, *refs):
    a_ref, own_ref = refs[:2]
    pieces = refs[2 : 2 + count]
    out_ref, other_ref, att_ref = refs[2 + count :]
    frames = a_ref.shape[0]
    local = own_ref.shape[-1]
    main, extra = load_packed(a_ref)
    size = main.shape[0]
    row = iota((size, size), 0)
    col = iota((size, size), 1)
    swap = jnp.where((row % frames) * ROWS + row // frames == col, 1.0, 0.0).astype(BF16)
    x = jnp.concatenate([dot(swap, main).astype(BF16), extra], axis=0)
    place_pieces(pieces, other_ref)
    for member, weights in enumerate((own_ref, other_ref)):
        q = (dot(x, weights[0]) * SCALE).astype(BF16)
        k = dot(x, weights[1]).astype(BF16)
        v = dot(x, weights[2]).astype(BF16)
        temporal_pairs(q, k, v, att_ref, member * local, frames)
    back = jnp.where((col % frames) * ROWS + col // frames == row, 1.0, 0.0).astype(BF16)
    store_packed(out_ref, dot(back, att_ref[:size, :]), att_ref[size:, :])


def middle_kernel(mine, count, *refs):
    r_ref, x_ref, own_ref = refs[:3]
    pieces = refs[3 : 3 + count]
    gain_ref, w_ref, mid_ref, qkv_ref, other_ref = refs[3 + count :]
    half = x_ref.shape[0] // 2
    place_pieces(pieces, other_ref)
    main, extra = load_packed(r_ref)
    att = jnp.concatenate([main, extra], axis=0)
    local = own_ref.shape[0]
    first, second = (own_ref, other_ref) if mine else (other_ref, own_ref)
    summed = dot(att[:, :local], first[...]) + dot(att[:, local:], second[...])
    mid = (x_ref[half_rows(half, mine), :].astype(F32) + summed).astype(BF16)
    mid_ref[...] = mid
    normed = layer_norm(mid.astype(F32), gain_ref[...])
    qkv_ref[0] = (dot(normed, w_ref[0]) * SCALE).astype(BF16)
    qkv_ref[1] = dot(normed, w_ref[1]).astype(BF16)
    qkv_ref[2] = dot(normed, w_ref[2]).astype(BF16)


def spatial_kernel(first, last, own_ref, other_ref, out_ref):
    half = own_ref.shape[1]
    low = iota((2 * half, LANES), 1) < HD
    for pair in range(first, last):
        lanes = slice(pair * LANES, (pair + 1) * LANES)
        keys = jnp.concatenate([own_ref[1, :, lanes], other_ref[1, :, lanes]], axis=0)
        vals = jnp.concatenate([own_ref[2, :, lanes], other_ref[2, :, lanes]], axis=0)
        zero = jnp.zeros_like(keys)
        one = jnp.ones_like(keys)
        keys_of = (jnp.where(low, keys, zero), jnp.where(low, zero, keys))
        vals_of = (jnp.where(low, vals, one), jnp.where(low, one, vals))
        for part, ref in enumerate((own_ref, other_ref)):
            q = ref[0, :, lanes]
            results = []
            for head in range(2):
                scores = dot_t(q, keys_of[head])
                weights = jnp.exp2(scores - jnp.max(scores, axis=-1, keepdims=True)).astype(BF16)
                results.append(dot(weights, vals_of[head]))
            here = low[:half]
            top = jnp.where(here, results[0], results[1])
            bottom = pltpu.roll(jnp.where(here, results[1], results[0]), HD, 1)
            at = (pair - first) * LANES
            out_ref[part * half : (part + 1) * half, at : at + LANES] = (top / bottom).astype(BF16)


def final_kernel(count, parts, *refs):
    mids = refs[:2]
    own = refs[2 : 2 + parts]
    partner = refs[2 + parts : 2 + 2 * parts]
    own_ref = refs[2 + 2 * parts]
    pieces = refs[3 + 2 * parts : 3 + 2 * parts + count]
    out_ref, other_ref = refs[3 + 2 * parts + count :]
    half = mids[0].shape[0]
    place_pieces(pieces, other_ref)
    for part, mine in enumerate((True, False)):
        here = slice(part * half, (part + 1) * half)
        there = slice((1 - part) * half, (2 - part) * half)
        total = mids[part][...].astype(F32)
        left = jnp.concatenate([ref[here, :] for ref in own], axis=1)
        right = jnp.concatenate([ref[there, :] for ref in partner], axis=1)
        total = total + dot(left, own_ref[...]) + dot(right, other_ref[...])
        out_ref[half_rows(half, mine), :] = total.astype(BF16)


def call(kernel, out, scratch=(), flops=0, limit=32):
    return pl.pallas_call(
        kernel,
        out_shape=out,
        scratch_shapes=list(scratch),
        compiler_params=pltpu.CompilerParams(vmem_limit_bytes=limit * 1024 * 1024),
        cost_estimate=pl.CostEstimate(flops=flops, bytes_accessed=4000000, transcendentals=0),
    )


def shape(*dims):
    return jax.ShapeDtypeStruct(dims, BF16)


def routes():
    devices = [(y, c, m) for y in (0, 1) for c in (0, 1) for m in (0, 1)]

    def index(y, c, m):
        return y * 4 + c * 2 + m

    across = [(index(y, c, m), index(1 - y, c, 1 - m)) for y, c, m in devices]
    beside = [(index(y, c, m), index(1 - y, c, m)) for y, c, m in devices]
    core = [(index(y, c, m), index(y, 1 - c, m)) for y, c, m in devices]
    return across, beside, core


def fetch_other(slices):
    across, beside, core = routes()
    axes = ("clip", "mp")
    mine = [lax.ppermute(piece, axes, across) for piece in slices]
    chip = [lax.ppermute(piece, axes, beside) for piece in mine]
    pair = [lax.ppermute(piece, axes, core) for piece in mine]
    last = [lax.ppermute(piece, axes, core) for piece in chip]
    return mine + pair + chip + last


def cut(weights, chunks):
    quarter = lax.axis_index("clip") ^ 2
    rows = weights.shape[-2] // (4 * chunks)
    lead = weights.ndim - 2
    out = []
    for chunk in range(chunks):
        start = [0] * lead + [(quarter * chunks + chunk) * rows, 0]
        out.append(lax.dynamic_slice(weights, start, weights.shape[:lead] + (rows, weights.shape[-1])))
    return out


def all_to_all(values):
    return lax.all_to_all(values, "tm", split_axis=0, concat_axis=0, tiled=True)


def shards(video, gain_time, qkv_time, proj_time, gain_space, qkv_space, proj_space):
    _, patches, width = video.shape
    frames = lax.axis_size("tm")
    local = qkv_time.shape[-1]
    half = patches // 2
    x = video[0]
    w_time = jnp.transpose(qkv_time, (1, 0, 2))
    w_space = jnp.transpose(qkv_space, (1, 0, 2))
    gain_time = gain_time.reshape(1, width)
    gain_space = gain_space.reshape(1, width)
    packed = shape(frames, ROWS, width + LANES)

    pieces = fetch_other(cut(w_time, 2))
    sent = call(norm_kernel, packed)(x, gain_time)
    arrived = all_to_all(sent)
    *pieces, arrived = lax.optimization_barrier((*pieces, arrived))

    attended = call(
        functools.partial(temporal_kernel, len(pieces)),
        packed,
        [pltpu.VMEM((3, width, local), BF16), pltpu.VMEM((half, width), BF16)],
        flops=2 * half * width * 3 * width,
    )(arrived, w_time, *pieces)
    proj_time_, proj_space_, _ = lax.optimization_barrier((proj_time, proj_space, pieces[-1]))
    time_pieces = fetch_other(cut(proj_time_, 1))
    space_pieces = fetch_other(cut(proj_space_, 1))
    back = all_to_all(attended)
    *both, back = lax.optimization_barrier((*time_pieces, *space_pieces, back))
    time_pieces, space_pieces = both[:4], both[4:]

    theirs = lax.ppermute(back, "mp", [(0, 1), (1, 0)])
    made = []
    for mine, values in ((True, back), (False, theirs)):
        made.append(
            call(
                functools.partial(middle_kernel, mine, 4),
                (shape(half, width), shape(3, half, local)),
                [pltpu.VMEM((local, width), BF16)],
                flops=2 * half * width * 4 * local,
            )(values, x, proj_time, *time_pieces, gain_space, w_space)
        )
    (mid_own, qkv_own), (mid_other, qkv_other) = made

    own, partner = [], []
    pairs = local // LANES
    for first in range(0, pairs, 2):
        part = call(
            functools.partial(spatial_kernel, first, first + 2),
            shape(patches, 2 * LANES),
            flops=4 * patches * patches * 2 * LANES,
        )(qkv_own, qkv_other)
        own.append(part)
        partner.append(lax.ppermute(part, "mp", [(0, 1), (1, 0)]))
    out = call(
        functools.partial(final_kernel, 4, len(own)),
        shape(patches, width),
        [pltpu.VMEM((local, width), BF16)],
        flops=2 * patches * width * width,
    )(mid_own, mid_other, *own, *partner, proj_space, *space_pieces)
    return out[None]


def solution(mesh):
    placed = (
        P(("clip", "tm"), None, None),
        P(),
        P(None, None, "mp"),
        P("mp", None),
        P(),
        P(None, None, "mp"),
        P("mp", None),
    )
    return jax.shard_map(
        shards, mesh=mesh, in_specs=placed, out_specs=P(("clip", "tm"), None, None), check_vma=False
    )
```

time: 283 us -> 141 us (0.50)
  waiting for transfers between devices: 115 us -> 41.5 us
  blocking collectives: 72.6 us -> 0 us
  starting transfers between devices: 8.12 us -> 45.8 us
  matrix products: 31.5 us -> 0 us
  Pallas kernels: 0 us -> 22.3 us
  between operations: 13.5 us -> 0.21 us
  other arithmetic: 10.5 us -> 0 us
    psum x2 -> x0, waiting for transfers between devices: 109 us -> none  [shards(): lax.psum(partial_sum.astype(jnp.bfloat16), 'mp').astype(jnp.float32)]
    all_to_all x3 -> x0, blocking collectives: 72.6 us -> none  [the longest x1 27 us: shards(): lax.all_to_all(triple[:, :, 0], 'tm', split_axis=1, concat_axis=0, tiled=...]
    ppermute x0 -> x19, waiting for transfers between devices: none -> 41.5 us  [the longest x2 12.6 us: shards(): partner.append(lax.ppermute(part, 'mp', [(0, 1), (1, 0)]))]
    ppermute x0 -> x19, starting transfers between devices: none -> 25.4 us  [the longest x4 9.75 us: fetch_other(): last = [lax.ppermute(piece, axes, core) for piece in chip]]
    pallas_call x0 -> x7, Pallas kernels: none -> 22.3 us  [the longest x2 6.91 us: shards(): call(functools.partial(spatial_kernel, first, first + 2), shape(patches,...]
    dot_general x7 -> x0, matrix products: 22.1 us -> none  [the longest x2 8.56 us: project(): jnp.dot(normed.reshape(-1, width), weights.reshape(width, 3 * local), pre...]
    unnamed x14 -> x78, local copies, waits for them, and re-layouts: 9.49 us -> 27.4 us
    all_to_all x1 -> x2, starting transfers between devices: 8.04 us -> 20.4 us  [all_to_all(): return lax.all_to_all(values, 'tm', split_axis=0, concat_axis=0, tiled=True)]
  transfers between devices with their start and end apart: 3 -> 21, of which waited for: 3 -> 9; matrix products, arithmetic and copies ran while one was open for 5% -> 1% of each run, Pallas kernels for 0% -> 3%
where the time goes in v1:
time: 141 us; the launch traced here: 140 us
  starting transfers between devices  45.8 us (32%)
  waiting for transfers between devices  41.5 us (29%)
  local copies, waits for them, and re-layouts  30.5 us (22%)
  Pallas kernels  22.3 us (16%)
    unnamed x78, local copies, waits for them, and re-layouts  27.4 us
    all_to_all x2, starting transfers between devices, all_to_all(): return lax.all_to_all(values, 'tm', split_axis=0, concat_axis=0, tiled=True)  20.4 us
    ppermute x2, waiting for transfers between devices, shards(): partner.append(lax.ppermute(part, 'mp', [(0, 1), (1, 0)]))  12.6 us
    ppermute x4, waiting for transfers between devices, fetch_other(): mine = [lax.ppermute(piece, axes, across) for piece in slices]  12.4 us
    ppermute x4, waiting for transfers between devices, fetch_other(): chip = [lax.ppermute(piece, axes, beside) for piece in mine]  10.8 us
    ppermute x4, starting transfers between devices, fetch_other(): last = [lax.ppermute(piece, axes, core) for piece in chip]  9.75 us
    pallas_call x2, Pallas kernels, shards(): call(functools.partial(spatial_kernel, first, first + 2), shape(patches,...  6.91 us
    ppermute x4, starting transfers between devices, fetch_other(): mine = [lax.ppermute(piece, axes, across) for piece in slices]  6.6 us
  transfers between devices with their start and end apart: 21, of which 9 were waited for; matrix products, arithmetic and copies ran while one was open for 1% of the time, Pallas kernels for 3%

profile of v1, /device:TPU:1, one launch (start us, length us, event | category | flops | bytes accessed | tf_op | source)
XLA Modules:
  0.0 140.3 jit_solution(1302872309891182467)
XLA Ops:
  0.0 1.2 dynamic-slice_bitcast_fusion
  1.2 3.7 %collective-permute-start.1 = (bf16[3,128,512]{2,1,0:T(8,128)(2,1)S(1)}, bf16[3,128,512]{2,1,0:T(8,128)(2,1)S(1)}, u32[]{:S(2)}, u32[]{:S(2)}) collective-permute-start(bf16[3,128,512]{2,1,0:T(8,128)(2,1)S(1)} %get-tuple-element.53), channel_id=1, source_target_pairs={{0,129},{1,128},{64,193},{65,192},{128,1},{129,0},{192,65},{193,64... | collective-permute-start | bytes 1179656 | tf_op jit(solution)/shard_map/ppermute | solution.py:251
  4.9 1.3 copy-done.1
  6.9 1.4 %shard_map.73 = bf16[32,8,1152]{2,1,0:T(8,128)(2,1)} custom-call(bf16[576,1024]{1,0:T(8,128)(2,1)S(1)} %bitcast.12, f32[1,1024]{1,0:T(1,128)S(1)} %bitcast.18), custom_call_target="tpu_custom_call" | custom-call | bytes 4000000 | tf_op jit(solution)/shard_map/pallas_call | solution.py:286
  8.3 11.0 %all-to-all-start = ((bf16[32,8,1152]{2,1,0:T(8,128)(2,1)}), bf16[32,8,1152]{2,1,0:T(8,128)(2,1)S(1)}, u32[]{:S(2)}, u32[]{:S(2)}) async-start(bf16[32,8,1152]{2,1,0:T(8,128)(2,1)} %shard_map.73), calls=%async_computation | async-start | bytes 1179648 | tf_op jit(solution)/shard_map/all_to_all | solution.py:270
  19.5 1.6 %collective-permute-done.refs_2_ = bf16[3,128,512]{2,1,0:T(8,128)(2,1)S(1)} collective-permute-done((bf16[3,128,512]{2,1,0:T(8,128)(2,1)S(1)}, bf16[3,128,512]{2,1,0:T(8,128)(2,1)S(1)}, u32[]{:S(2)}, u32[]{:S(2)}) %collective-permute-start) | collective-permute-done | bytes 393248 | tf_op jit(solution)/shard_map/ppermute | solution.py:251
  21.8 1.8 %collective-permute-start.3 = (bf16[3,128,512]{2,1,0:T(8,128)(2,1)S(1)}, bf16[3,128,512]{2,1,0:T(8,128)(2,1)S(1)}, u32[]{:S(2)}, u32[]{:S(2)}) collective-permute-start(bf16[3,128,512]{2,1,0:T(8,128)(2,1)S(1)} %collective-permute-done.1.refs_3_), channel_id=1, source_target_pairs={{0,64},{1,65},{64,0},{65,1},{128,192},{129,193},{192,128},{193,129... | collective-permute-start | bytes 1179656 | tf_op jit(solution)/shard_map/ppermute | solution.py:253
  24.4 4.3 %collective-permute-done.5.refs_7_ = bf16[3,128,512]{2,1,0:T(8,128)(2,1)S(1)} collective-permute-done((bf16[3,128,512]{2,1,0:T(8,128)(2,1)S(1)}, bf16[3,128,512]{2,1,0:T(8,128)(2,1)S(1)}, u32[]{:S(2)}, u32[]{:S(2)}) %collective-permute-start.5) | collective-permute-done | bytes 393248 | tf_op jit(solution)/shard_map/ppermute | solution.py:252
  28.7 4.2 %collective-permute-start.7 = (bf16[3,128,512]{2,1,0:T(8,128)(2,1)S(1)}, bf16[3,128,512]{2,1,0:T(8,128)(2,1)S(1)}, u32[]{:S(2)}, u32[]{:S(2)}) collective-permute-start(bf16[3,128,512]{2,1,0:T(8,128)(2,1)S(1)} %collective-permute-done.5.refs_7_), channel_id=1, source_target_pairs={{0,64},{1,65},{64,0},{65,1},{128,192},{129,193},{192,128},{193,129... | collective-permute-start | bytes 1179656 | tf_op jit(solution)/shard_map/ppermute | solution.py:254
  33.6 3.5 %collective-permute-done.4.refs_6_ = bf16[3,128,512]{2,1,0:T(8,128)(2,1)S(1)} collective-permute-done((bf16[3,128,512]{2,1,0:T(8,128)(2,1)S(1)}, bf16[3,128,512]{2,1,0:T(8,128)(2,1)S(1)}, u32[]{:S(2)}, u32[]{:S(2)}) %collective-permute-start.4) | collective-permute-done | bytes 393248 | tf_op jit(solution)/shard_map/ppermute | solution.py:252
  37.1 2.3 %collective-permute-start.6 = (bf16[3,128,512]{2,1,0:T(8,128)(2,1)S(1)}, bf16[3,128,512]{2,1,0:T(8,128)(2,1)}, u32[]{:S(2)}, u32[]{:S(2)}) collective-permute-start(bf16[3,128,512]{2,1,0:T(8,128)(2,1)S(1)} %collective-permute-done.4.refs_6_), channel_id=1, source_target_pairs={{0,64},{1,65},{64,0},{65,1},{128,192},{129,193},{192,128},{193,129... | collective-permute-start | bytes 1179656 | tf_op jit(solution)/shard_map/ppermute | solution.py:254
  43.3 1.9 %copy-done.4 = bf16[1024,3,512]{2,0,1:T(8,128)(2,1)S(1)} copy-done((bf16[1024,3,512]{2,0,1:T(8,128)(2,1)S(1)}, bf16[1024,3,512]{2,0,1:T(8,128)(2,1)}, u32[]{:S(2)}) %copy-start.4) | copy-done | bytes 3145752
  52.2 6.0 %shard_map.74 = bf16[32,8,1152]{2,1,0:T(8,128)(2,1)S(1)} custom-call(bf16[32,8,1152]{2,1,0:T(8,128)(2,1)S(1)} %copy-done.7, bf16[3,1024,512]{2,1,0:T(8,128)(2,1)S(1)} %bitcast.15, bf16[3,128,512]{2,1,0:T(8,128)(2,1)S(1)} %copy-done.18, bf16[3,128,512]{2,1,0:T(8,128)(2,1)S(1)} %collective-permute-done.1.refs_3_, bf16[3,128,512]{2,1,0:T(8,128)(2,1)S(1)} %copy-done.26, ...), custom_call_target="tpu_custom_call" | custom-call | flops 1811939328 | bytes 4000000 | tf_op jit(solution)/shard_map/pallas_call | solution.py:290
  59.1 9.3 %all-to-all-start.1 = ((bf16[32,8,1152]{2,1,0:T(8,128)(2,1)}), bf16[32,8,1152]{2,1,0:T(8,128)(2,1)}, u32[]{:S(2)}, u32[]{:S(2)}) async-start(bf16[32,8,1152]{2,1,0:T(8,128)(2,1)} %copy-done.5), calls=%async_computation.1 | async-start | bytes 1179648 | tf_op jit(solution)/shard_map/all_to_all | solution.py:270
  69.4 2.7 %collective-permute-start.12 = (bf16[128,1024]{1,0:T(8,128)(2,1)S(1)}, bf16[128,1024]{1,0:T(8,128)(2,1)S(1)}, u32[]{:S(2)}, u32[]{:S(2)}) collective-permute-start(bf16[128,1024]{1,0:T(8,128)(2,1)S(1)} %constant_dynamic-slice_fusion), channel_id=1, source_target_pairs={{0,129},{1,128},{64,193},{65,192},{128,1},{129,0},{192,65},{193,64... | collective-permute-start | bytes 786440 | tf_op jit(solution)/shard_map/ppermute | solution.py:251
  73.2 5.2 %collective-permute-done.12.refs_7_ = bf16[128,1024]{1,0:T(8,128)(2,1)S(1)} collective-permute-done((bf16[128,1024]{1,0:T(8,128)(2,1)S(1)}, bf16[128,1024]{1,0:T(8,128)(2,1)S(1)}, u32[]{:S(2)}, u32[]{:S(2)}) %collective-permute-start.12) | collective-permute-done | bytes 262176 | tf_op jit(solution)/shard_map/ppermute | solution.py:251
  78.4 5.6 %collective-permute-done.8.refs_3_ = bf16[128,1024]{1,0:T(8,128)(2,1)S(1)} collective-permute-done((bf16[128,1024]{1,0:T(8,128)(2,1)S(1)}, bf16[128,1024]{1,0:T(8,128)(2,1)S(1)}, u32[]{:S(2)}, u32[]{:S(2)}) %collective-permute-start.8) | collective-permute-done | bytes 262176 | tf_op jit(solution)/shard_map/ppermute | solution.py:251
  85.7 1.4 collective-permute-start.15
  87.8 3.0 %collective-permute-done.10.refs_5_ = bf16[128,1024]{1,0:T(8,128)(2,1)S(1)} collective-permute-done((bf16[128,1024]{1,0:T(8,128)(2,1)S(1)}, bf16[128,1024]{1,0:T(8,128)(2,1)S(1)}, u32[]{:S(2)}, u32[]{:S(2)}) %collective-permute-start.10) | collective-permute-done | bytes 262176 | tf_op jit(solution)/shard_map/ppermute | solution.py:252
  90.8 1.9 %collective-permute-start.11 = (bf16[128,1024]{1,0:T(8,128)(2,1)S(1)}, bf16[128,1024]{1,0:T(8,128)(2,1)S(1)}, u32[]{:S(2)}, u32[]{:S(2)}) collective-permute-start(bf16[128,1024]{1,0:T(8,128)(2,1)S(1)} %collective-permute-done.10.refs_5_), channel_id=1, source_target_pairs={{0,64},{1,65},{64,0},{65,1},{128,192},{129,193},{192,128},{193,129... | collective-permute-start | bytes 786440 | tf_op jit(solution)/shard_map/ppermute | solution.py:254
  96.3 2.3 %collective-permute-start.16 = (bf16[32,8,1152]{2,1,0:T(8,128)(2,1)}, bf16[32,8,1152]{2,1,0:T(8,128)(2,1)S(1)}, u32[]{:S(2)}, u32[]{:S(2)}) collective-permute-start(bf16[32,8,1152]{2,1,0:T(8,128)(2,1)} %all-to-all-done.1.refs_0_), channel_id=1, source_target_pairs={{0,1},{1,0},{2,3},{3,2},{4,5},{5,4},{6,7},{7,6},{8,9},{9,8},{10,11... | collective-permute-start | bytes 1769480 | tf_op jit(solution)/shard_map/ppermute | solution.py:303
  98.6 1.3 copy-done.2
  99.9 1.2 copy-done.3
  103.9 3.3 %shard_map.75 = (bf16[288,1024]{1,0:T(8,128)(2,1)S(1)}, bf16[3,288,512]{2,1,0:T(8,128)(2,1)S(1)}) custom-call(bf16[32,8,1152]{2,1,0:T(8,128)(2,1)} %all-to-all-done.1.refs_0_, bf16[576,1024]{1,0:T(8,128)(2,1)S(1)} %bitcast.13, bf16[512,1024]{1,0:T(8,128)(2,1)S(1)} %copy-done.3, bf16[128,1024]{1,0:T(8,128)(2,1)S(1)} %collective-permute-done.8.refs_3_, ...), custom_call_target="tpu_custom_call" | custom-call | flops 1207959552 | bytes 4000000 | tf_op jit(solution)/shard_map/pallas_call | solution.py:307
  107.3 5.7 %collective-permute-done.16.refs_0_ = bf16[32,8,1152]{2,1,0:T(8,128)(2,1)S(1)} collective-permute-done((bf16[32,8,1152]{2,1,0:T(8,128)(2,1)}, bf16[32,8,1152]{2,1,0:T(8,128)(2,1)S(1)}, u32[]{:S(2)}, u32[]{:S(2)}) %collective-permute-start.16) | collective-permute-done | bytes 589856 | tf_op jit(solution)/shard_map/ppermute | solution.py:303
  113.0 2.2 %shard_map.76 = (bf16[288,1024]{1,0:T(8,128)(2,1)S(1)}, bf16[3,288,512]{2,1,0:T(8,128)(2,1)S(1)}) custom-call(bf16[32,8,1152]{2,1,0:T(8,128)(2,1)S(1)} %collective-permute-done.16.refs_0_, bf16[576,1024]{1,0:T(8,128)(2,1)S(1)} %bitcast.14, bf16[512,1024]{1,0:T(8,128)(2,1)S(1)} %copy-done.3, bf16[128,1024]{1,0:T(8,128)(2,1)S(1)} %collective-permute-done.8.refs_3_, ...), custom_call_target="tpu_custom_call" | custom-call | flops 1207959552 | bytes 4000000 | tf_op jit(solution)/shard_map/pallas_call | solution.py:307
  115.2 3.5 %shard_map.78.refs_3_ = bf16[576,256]{1,0:T(8,128)(2,1)S(1)} custom-call(bf16[3,288,512]{2,1,0:T(8,128)(2,1)S(1)} %get-tuple-element.47.own_ref, bf16[3,288,512]{2,1,0:T(8,128)(2,1)S(1)} %get-tuple-element.48.other_ref), custom_call_target="tpu_custom_call" | custom-call | flops 339738624 | bytes 4000000 | tf_op jit(solution)/shard_map/pallas_call | solution.py:319
  118.7 3.5 %shard_map.77.refs_2_ = bf16[576,256]{1,0:T(8,128)(2,1)S(1)} custom-call(bf16[3,288,512]{2,1,0:T(8,128)(2,1)S(1)} %get-tuple-element.47.own_ref, bf16[3,288,512]{2,1,0:T(8,128)(2,1)S(1)} %get-tuple-element.48.other_ref), custom_call_target="tpu_custom_call" | custom-call | flops 339738624 | bytes 4000000 | tf_op jit(solution)/shard_map/pallas_call | solution.py:319
  122.1 2.4 %collective-permute-start.17 = (bf16[576,256]{1,0:T(8,128)(2,1)S(1)}, bf16[576,256]{1,0:T(8,128)(2,1)S(1)}, u32[]{:S(2)}, u32[]{:S(2)}) collective-permute-start(bf16[576,256]{1,0:T(8,128)(2,1)S(1)} %shard_map.77.refs_2_), channel_id=1, source_target_pairs={{0,1},{1,0},{2,3},{3,2},{4,5},{5,4},{6,7},{7,6},{8,9},{9,8},{10,11... | collective-permute-start | bytes 884744 | tf_op jit(solution)/shard_map/ppermute | solution.py:325
  125.2 6.3 %collective-permute-done.17.refs_4_ = bf16[576,256]{1,0:T(8,128)(2,1)S(1)} collective-permute-done((bf16[576,256]{1,0:T(8,128)(2,1)S(1)}, bf16[576,256]{1,0:T(8,128)(2,1)S(1)}, u32[]{:S(2)}, u32[]{:S(2)}) %collective-permute-start.17) | collective-permute-done | bytes 294944 | tf_op jit(solution)/shard_map/ppermute | solution.py:325
  131.5 6.3 %collective-permute-done.18.refs_5_ = bf16[576,256]{1,0:T(8,128)(2,1)S(1)} collective-permute-done((bf16[576,256]{1,0:T(8,128)(2,1)S(1)}, bf16[576,256]{1,0:T(8,128)(2,1)S(1)}, u32[]{:S(2)}, u32[]{:S(2)}) %collective-permute-start.18) | collective-permute-done | bytes 294944 | tf_op jit(solution)/shard_map/ppermute | solution.py:325
  137.8 2.5 %shard_map.79 = bf16[576,1024]{1,0:T(8,128)(2,1)} custom-call(bf16[288,1024]{1,0:T(8,128)(2,1)S(1)} %get-tuple-element.45.refs_0_, bf16[288,1024]{1,0:T(8,128)(2,1)S(1)} %get-tuple-element.46.refs_1_, bf16[576,256]{1,0:T(8,128)(2,1)S(1)} %shard_map.77.refs_2_, bf16[576,256]{1,0:T(8,128)(2,1)S(1)} %shard_map.78.refs_3_, ...), custom_call_target="tpu_custom_call" | custom-call | flops 1207959552 | bytes 4000000 | tf_op jit(solution)/shard_map/pallas_call | solution.py:326
  (98 shorter events, 26.5 us)
Async XLA Ops:
  1.2 18.2 %collective-permute-start.1 = (bf16[3,128,512]{2,1,0:T(8,128)(2,1)S(1)}, bf16[3,128,512]{2,1,0:T(8,128)(2,1)S(1)}, u32[]{:S(2)}, u32[]{:S(2)}) collective-permute-start(bf16[3,128,512]{2,1,0:T(8,128)(2,1)S(1)} %get-tuple-element.53), channel_id=1, source_target_pairs={{0,129},{1,128},{64,193},{65,192},{128,1},{129,0},{192,65},{193,64... | collective-permute-start | bytes 1179656 | tf_op jit(solution)/shard_map/ppermute | solution.py:251
  4.8 16.2 %collective-permute-start = (bf16[3,128,512]{2,1,0:T(8,128)(2,1)S(1)}, bf16[3,128,512]{2,1,0:T(8,128)(2,1)S(1)}, u32[]{:S(2)}, u32[]{:S(2)}) collective-permute-start(bf16[3,128,512]{2,1,0:T(8,128)(2,1)S(1)} %get-tuple-element.54), channel_id=1, source_target_pairs={{0,129},{1,128},{64,193},{65,192},{128,1},{129,0},{192,65},{193,64... | collective-permute-start | bytes 1179656 | tf_op jit(solution)/shard_map/ppermute | solution.py:251
  8.3 33.4 %all-to-all-start = ((bf16[32,8,1152]{2,1,0:T(8,128)(2,1)}), bf16[32,8,1152]{2,1,0:T(8,128)(2,1)S(1)}, u32[]{:S(2)}, u32[]{:S(2)}) async-start(bf16[32,8,1152]{2,1,0:T(8,128)(2,1)} %shard_map.73), calls=%async_computation | async-start | bytes 1179648 | tf_op jit(solution)/shard_map/all_to_all | solution.py:270
  19.4 9.3 %collective-permute-start.5 = (bf16[3,128,512]{2,1,0:T(8,128)(2,1)S(1)}, bf16[3,128,512]{2,1,0:T(8,128)(2,1)S(1)}, u32[]{:S(2)}, u32[]{:S(2)}) collective-permute-start(bf16[3,128,512]{2,1,0:T(8,128)(2,1)S(1)} %collective-permute-done.1.refs_3_), channel_id=1, source_target_pairs={{0,128},{1,129},{64,192},{65,193},{128,0},{129,1},{192,64},{193,65... | collective-permute-start | bytes 1179656 | tf_op jit(solution)/shard_map/ppermute | solution.py:252
  21.0 16.1 %collective-permute-start.4 = (bf16[3,128,512]{2,1,0:T(8,128)(2,1)S(1)}, bf16[3,128,512]{2,1,0:T(8,128)(2,1)S(1)}, u32[]{:S(2)}, u32[]{:S(2)}) collective-permute-start(bf16[3,128,512]{2,1,0:T(8,128)(2,1)S(1)} %collective-permute-done.refs_2_), channel_id=1, source_target_pairs={{0,128},{1,129},{64,192},{65,193},{128,0},{129,1},{192,64},{193,65... | collective-permute-start | bytes 1179656 | tf_op jit(solution)/shard_map/ppermute | solution.py:252
  21.8 18.4 %collective-permute-start.3 = (bf16[3,128,512]{2,1,0:T(8,128)(2,1)S(1)}, bf16[3,128,512]{2,1,0:T(8,128)(2,1)S(1)}, u32[]{:S(2)}, u32[]{:S(2)}) collective-permute-start(bf16[3,128,512]{2,1,0:T(8,128)(2,1)S(1)} %collective-permute-done.1.refs_3_), channel_id=1, source_target_pairs={{0,64},{1,65},{64,0},{65,1},{128,192},{129,193},{192,128},{193,129... | collective-permute-start | bytes 1179656 | tf_op jit(solution)/shard_map/ppermute | solution.py:253
  23.6 17.3 %collective-permute-start.2 = (bf16[3,128,512]{2,1,0:T(8,128)(2,1)S(1)}, bf16[3,128,512]{2,1,0:T(8,128)(2,1)S(1)}, u32[]{:S(2)}, u32[]{:S(2)}) collective-permute-start(bf16[3,128,512]{2,1,0:T(8,128)(2,1)S(1)} %collective-permute-done.refs_2_), channel_id=1, source_target_pairs={{0,64},{1,65},{64,0},{65,1},{128,192},{129,193},{192,128},{193,129... | collective-permute-start | bytes 1179656 | tf_op jit(solution)/shard_map/ppermute | solution.py:253
  28.7 13.8 %collective-permute-start.7 = (bf16[3,128,512]{2,1,0:T(8,128)(2,1)S(1)}, bf16[3,128,512]{2,1,0:T(8,128)(2,1)S(1)}, u32[]{:S(2)}, u32[]{:S(2)}) collective-permute-start(bf16[3,128,512]{2,1,0:T(8,128)(2,1)S(1)} %collective-permute-done.5.refs_7_), channel_id=1, source_target_pairs={{0,64},{1,65},{64,0},{65,1},{128,192},{129,193},{192,128},{193,129... | collective-permute-start | bytes 1179656 | tf_op jit(solution)/shard_map/ppermute | solution.py:254
  37.1 6.2 %collective-permute-start.6 = (bf16[3,128,512]{2,1,0:T(8,128)(2,1)S(1)}, bf16[3,128,512]{2,1,0:T(8,128)(2,1)}, u32[]{:S(2)}, u32[]{:S(2)}) collective-permute-start(bf16[3,128,512]{2,1,0:T(8,128)(2,1)S(1)} %collective-permute-done.4.refs_6_), channel_id=1, source_target_pairs={{0,64},{1,65},{64,0},{65,1},{128,192},{129,193},{192,128},{193,129... | collective-permute-start | bytes 1179656 | tf_op jit(solution)/shard_map/ppermute | solution.py:254
  43.3 1.9 %copy-start.4 = (bf16[1024,3,512]{2,0,1:T(8,128)(2,1)S(1)}, bf16[1024,3,512]{2,0,1:T(8,128)(2,1)}, u32[]{:S(2)}) copy-start(bf16[1024,3,512]{2,0,1:T(8,128)(2,1)} %param.9) | copy-start | bytes 9437188
  52.2 46.4 %copy-start = (bf16[1024,3,512]{2,0,1:T(8,128)(2,1)S(1)}, bf16[1024,3,512]{2,0,1:T(8,128)(2,1)}, u32[]{:S(2)}) copy-start(bf16[1024,3,512]{2,0,1:T(8,128)(2,1)} %param.12) | copy-start | bytes 9437188
  52.2 46.4 %copy-start.37 = (f32[1024]{0:T(1024)S(1)}, f32[1024]{0:T(1024)}, u32[]{:S(2)}) copy-start(f32[1024]{0:T(1024)} %param.11) | copy-start | bytes 12292
  59.1 37.2 %all-to-all-start.1 = ((bf16[32,8,1152]{2,1,0:T(8,128)(2,1)}), bf16[32,8,1152]{2,1,0:T(8,128)(2,1)}, u32[]{:S(2)}, u32[]{:S(2)}) async-start(bf16[32,8,1152]{2,1,0:T(8,128)(2,1)} %copy-done.5), calls=%async_computation.1 | async-start | bytes 1179648 | tf_op jit(solution)/shard_map/all_to_all | solution.py:270
  69.4 9.0 %collective-permute-start.12 = (bf16[128,1024]{1,0:T(8,128)(2,1)S(1)}, bf16[128,1024]{1,0:T(8,128)(2,1)S(1)}, u32[]{:S(2)}, u32[]{:S(2)}) collective-permute-start(bf16[128,1024]{1,0:T(8,128)(2,1)S(1)} %constant_dynamic-slice_fusion), channel_id=1, source_target_pairs={{0,129},{1,128},{64,193},{65,192},{128,1},{129,0},{192,65},{193,64... | collective-permute-start | bytes 786440 | tf_op jit(solution)/shard_map/ppermute | solution.py:251
  73.0 11.0 %collective-permute-start.8 = (bf16[128,1024]{1,0:T(8,128)(2,1)S(1)}, bf16[128,1024]{1,0:T(8,128)(2,1)S(1)}, u32[]{:S(2)}, u32[]{:S(2)}) collective-permute-start(bf16[128,1024]{1,0:T(8,128)(2,1)S(1)} %constant_dynamic-slice_fusion.1), channel_id=1, source_target_pairs={{0,129},{1,128},{64,193},{65,192},{128,1},{129,0},{192,65},{193,64... | collective-permute-start | bytes 786440 | tf_op jit(solution)/shard_map/ppermute | solution.py:251
  78.4 7.3 %collective-permute-start.14 = (bf16[128,1024]{1,0:T(8,128)(2,1)S(1)}, bf16[128,1024]{1,0:T(8,128)(2,1)S(1)}, u32[]{:S(2)}, u32[]{:S(2)}) collective-permute-start(bf16[128,1024]{1,0:T(8,128)(2,1)S(1)} %collective-permute-done.12.refs_7_), channel_id=1, source_target_pairs={{0,128},{1,129},{64,192},{65,193},{128,0},{129,1},{192,64},{193,65... | collective-permute-start | bytes 786440 | tf_op jit(solution)/shard_map/ppermute | solution.py:252
  84.0 6.8 %collective-permute-start.10 = (bf16[128,1024]{1,0:T(8,128)(2,1)S(1)}, bf16[128,1024]{1,0:T(8,128)(2,1)S(1)}, u32[]{:S(2)}, u32[]{:S(2)}) collective-permute-start(bf16[128,1024]{1,0:T(8,128)(2,1)S(1)} %collective-permute-done.8.refs_3_), channel_id=1, source_target_pairs={{0,128},{1,129},{64,192},{65,193},{128,0},{129,1},{192,64},{193,65... | collective-permute-start | bytes 786440 | tf_op jit(solution)/shard_map/ppermute | solution.py:252
  84.0 9.4 %collective-permute-start.13 = (bf16[128,1024]{1,0:T(8,128)(2,1)S(1)}, bf16[128,1024]{1,0:T(8,128)(2,1)S(1)}, u32[]{:S(2)}, u32[]{:S(2)}) collective-permute-start(bf16[128,1024]{1,0:T(8,128)(2,1)S(1)} %collective-permute-done.12.refs_7_), channel_id=1, source_target_pairs={{0,64},{1,65},{64,0},{65,1},{128,192},{129,193},{192,128},{193,129... | collective-permute-start | bytes 786440 | tf_op jit(solution)/shard_map/ppermute | solution.py:253
  85.7 8.4 %collective-permute-start.9 = (bf16[128,1024]{1,0:T(8,128)(2,1)S(1)}, bf16[128,1024]{1,0:T(8,128)(2,1)S(1)}, u32[]{:S(2)}, u32[]{:S(2)}) collective-permute-start(bf16[128,1024]{1,0:T(8,128)(2,1)S(1)} %collective-permute-done.8.refs_3_), channel_id=1, source_target_pairs={{0,64},{1,65},{64,0},{65,1},{128,192},{129,193},{192,128},{193,129... | collective-permute-start | bytes 786440 | tf_op jit(solution)/shard_map/ppermute | solution.py:253
  85.7 9.1 %collective-permute-start.15 = (bf16[128,1024]{1,0:T(8,128)(2,1)S(1)}, bf16[128,1024]{1,0:T(8,128)(2,1)S(1)}, u32[]{:S(2)}, u32[]{:S(2)}) collective-permute-start(bf16[128,1024]{1,0:T(8,128)(2,1)S(1)} %collective-permute-done.14.refs_9_), channel_id=1, source_target_pairs={{0,64},{1,65},{64,0},{65,1},{128,192},{129,193},{192,128},{193,129... | collective-permute-start | bytes 786440 | tf_op jit(solution)/shard_map/ppermute | solution.py:254
  90.8 4.7 %collective-permute-start.11 = (bf16[128,1024]{1,0:T(8,128)(2,1)S(1)}, bf16[128,1024]{1,0:T(8,128)(2,1)S(1)}, u32[]{:S(2)}, u32[]{:S(2)}) collective-permute-start(bf16[128,1024]{1,0:T(8,128)(2,1)S(1)} %collective-permute-done.10.refs_5_), channel_id=1, source_target_pairs={{0,64},{1,65},{64,0},{65,1},{128,192},{129,193},{192,128},{193,129... | collective-permute-start | bytes 786440 | tf_op jit(solution)/shard_map/ppermute | solution.py:254
  96.3 16.7 %collective-permute-start.16 = (bf16[32,8,1152]{2,1,0:T(8,128)(2,1)}, bf16[32,8,1152]{2,1,0:T(8,128)(2,1)S(1)}, u32[]{:S(2)}, u32[]{:S(2)}) collective-permute-start(bf16[32,8,1152]{2,1,0:T(8,128)(2,1)} %all-to-all-done.1.refs_0_), channel_id=1, source_target_pairs={{0,1},{1,0},{2,3},{3,2},{4,5},{5,4},{6,7},{7,6},{8,9},{9,8},{10,11... | collective-permute-start | bytes 1769480 | tf_op jit(solution)/shard_map/ppermute | solution.py:303
  98.6 1.3 copy-start.2
  103.9 9.0 %copy-start.11 = (bf16[128,1024]{1,0:T(8,128)(2,1)S(1)}, bf16[128,1024]{1,0:T(8,128)(2,1)}, u32[]{:S(2)}) copy-start(bf16[128,1024]{1,0:T(8,128)(2,1)} %copy-done.9) | copy-start | bytes 786436
  103.9 9.0 %copy-start.16 = (bf16[128,1024]{1,0:T(8,128)(2,1)S(1)}, bf16[128,1024]{1,0:T(8,128)(2,1)}, u32[]{:S(2)}) copy-start(bf16[128,1024]{1,0:T(8,128)(2,1)} %copy-done.14) | copy-start | bytes 786436
  115.2 22.6 %copy-start.8 = (bf16[512,1024]{1,0:T(8,128)(2,1)S(1)}, bf16[512,1024]{1,0:T(8,128)(2,1)}, u32[]{:S(2)}) copy-start(bf16[512,1024]{1,0:T(8,128)(2,1)} %refs_6_.1) | copy-start | bytes 3145732
  115.2 22.6 %copy-start.30 = (bf16[128,1024]{1,0:T(8,128)(2,1)S(1)}, bf16[128,1024]{1,0:T(8,128)(2,1)}, u32[]{:S(2)}) copy-start(bf16[128,1024]{1,0:T(8,128)(2,1)} %copy-done.29) | copy-start | bytes 786436
  115.2 22.6 %copy-start.32 = (bf16[128,1024]{1,0:T(8,128)(2,1)S(1)}, bf16[128,1024]{1,0:T(8,128)(2,1)}, u32[]{:S(2)}) copy-start(bf16[128,1024]{1,0:T(8,128)(2,1)} %copy-done.31) | copy-start | bytes 786436
  115.2 22.6 %copy-start.34 = (bf16[128,1024]{1,0:T(8,128)(2,1)S(1)}, bf16[128,1024]{1,0:T(8,128)(2,1)}, u32[]{:S(2)}) copy-start(bf16[128,1024]{1,0:T(8,128)(2,1)} %copy-done.33) | copy-start | bytes 786436
  115.2 22.6 %copy-start.36 = (bf16[128,1024]{1,0:T(8,128)(2,1)S(1)}, bf16[128,1024]{1,0:T(8,128)(2,1)}, u32[]{:S(2)}) copy-start(bf16[128,1024]{1,0:T(8,128)(2,1)} %copy-done.35) | copy-start | bytes 786436
  122.1 9.3 %collective-permute-start.17 = (bf16[576,256]{1,0:T(8,128)(2,1)S(1)}, bf16[576,256]{1,0:T(8,128)(2,1)S(1)}, u32[]{:S(2)}, u32[]{:S(2)}) collective-permute-start(bf16[576,256]{1,0:T(8,128)(2,1)S(1)} %shard_map.77.refs_2_), channel_id=1, source_target_pairs={{0,1},{1,0},{2,3},{3,2},{4,5},{5,4},{6,7},{7,6},{8,9},{9,8},{10,11... | collective-permute-start | bytes 884744 | tf_op jit(solution)/shard_map/ppermute | solution.py:325
  124.5 13.3 %collective-permute-start.18 = (bf16[576,256]{1,0:T(8,128)(2,1)S(1)}, bf16[576,256]{1,0:T(8,128)(2,1)S(1)}, u32[]{:S(2)}, u32[]{:S(2)}) collective-permute-start(bf16[576,256]{1,0:T(8,128)(2,1)S(1)} %shard_map.78.refs_3_), channel_id=1, source_target_pairs={{0,1},{1,0},{2,3},{3,2},{4,5},{5,4},{6,7},{7,6},{8,9},{9,8},{10,11... | collective-permute-start | bytes 884744 | tf_op jit(solution)/shard_map/ppermute | solution.py:325
  (28 other events, 24.2 us)

commit v2 on v1

--- a/solution.py
+++ b/solution.py
@@ -16,6 +16,8 @@
 SCALE = math.log2(math.e) / math.sqrt(HD)
 EPS = 1e-05
 MASKED = -1e30
+C_NORM = 4
+C_JOIN = 4
 
 
 def dot(left, right):
@@ -81,28 +83,66 @@
     return pl.ds(pl.multiple_of(place * count, 32), count)
 
 
-def norm_kernel(x_ref, gain_ref, out_ref):
-    half = x_ref.shape[0] // 2
-    frames = out_ref.shape[0]
-    x = x_ref[half_rows(half, True), :].astype(F32)
-    normed = layer_norm(x, gain_ref[...])
-    main = frames * ROWS
+def cut_kernel(w_ref, out_ref, sem):
+    rows = out_ref.shape[1]
+    start = (lax.axis_index("clip") ^ 2) * rows
+    copy = pltpu.make_async_copy(w_ref.at[:, pl.ds(pl.multiple_of(start, 16), rows), :], out_ref, sem)
+    copy.start()
+    copy.wait()
+
+
+def cut_proj_kernel(time_ref, space_ref, time_out, space_out, sems):
+    rows = time_out.shape[0]
+    start = (lax.axis_index("clip") ^ 2) * rows
+    place = pl.ds(pl.multiple_of(start, rows), rows)
+    copies = [
+        pltpu.make_async_copy(time_ref.at[place, :], time_out, sems.at[0]),
+        pltpu.make_async_copy(space_ref.at[place, :], space_out, sems.at[1]),
+    ]
+    for copy in copies:
+        copy.start()
+    for copy in copies:
+        copy.wait()
+
+
+def norm_kernel(x_ref, gain_ref, w_ref, out_ref, cut_ref, held, gain, sems):
+    half = held.shape[0]
+    main = out_ref.shape[0] * ROWS
+    rows = cut_ref.shape[1]
+    start = w_ref.shape[1] - 2 * rows + (lax.axis_index("clip") % 2) * rows
+    place = pl.ds(pl.multiple_of(start, 16), rows)
+    copies = [
+        pltpu.make_async_copy(x_ref.at[half_rows(half, True), :], held, sems.at[0]),
+        pltpu.make_async_copy(gain_ref, gain, sems.at[1]),
+        pltpu.make_async_copy(w_ref.at[:, place, :], cut_ref, sems.at[2]),
+    ]
+    for copy in copies:
+        copy.start()
+    copies[0].wait()
+    copies[1].wait()
+    normed = layer_norm(held[...].astype(F32), gain[...])
     store_packed(out_ref, normed[:main].astype(F32), normed[main:])
-
-
-def place_pieces(pieces, target):
+    copies[2].wait()
+
+
+def piece_copies(pieces, starts, target, sems):
+    copies = []
+    for at, (piece, start) in enumerate(zip(pieces, starts, strict=True)):
+        place = pl.ds(pl.multiple_of(start, 16), piece.shape[-2])
+        spot = target.at[:, place, :] if len(target.shape) == 3 else target.at[place, :]
+        copies.append(pltpu.make_async_copy(piece, spot, sems.at[at]))
+    return copies
+
+
+def part_starts(first, second):
     clip = lax.axis_index("clip")
-    count = len(pieces) // 4
-    rows = target.shape[-2] // len(pieces)
-    for distance in range(4):
-        quarter = clip ^ distance
-        for chunk in range(count):
-            start = pl.multiple_of((quarter * count + chunk) * rows, rows)
-            piece = pieces[distance * count + chunk]
-            if len(target.shape) == 3:
-                target[:, pl.ds(start, rows), :] = piece[...]
-            else:
-                target[pl.ds(start, rows), :] = piece[...]
+    starts = [(clip ^ distance) * first for distance in range(4)]
+    return starts + [4 * first + ((clip % 2) ^ distance) * second for distance in range(2)]
+
+
+def quarter_starts(rows):
+    clip = lax.axis_index("clip")
+    return [(clip ^ distance) * rows for distance in range(4)]
 
 
 def temporal_pairs(q, k, v, out, at, frames):
@@ -134,40 +174,71 @@
             out[start : start + count, at + pair * LANES : at + (pair + 1) * LANES] = result.astype(BF16)
 
 
-def temporal_kernel(count, *refs):
-    a_ref, own_ref = refs[:2]
-    pieces = refs[2 : 2 + count]
-    out_ref, other_ref, att_ref = refs[2 + count :]
-    frames = a_ref.shape[0]
-    local = own_ref.shape[-1]
-    main, extra = load_packed(a_ref)
+def temporal_heads(x, w_ref, att_ref, frames, waits=None):
+    made = []
+    for member in range(3):
+        if waits:
+            waits[member].wait()
+        flat = dot(x, w_ref[member])
+        made.append((flat * SCALE if member == 0 else flat).astype(BF16))
+    temporal_pairs(*made, att_ref, 0, frames)
+
+
+def own_heads_kernel(a_ref, w_ref, x_out, att_out, held, w_held, sems):
+    copies = [pltpu.make_async_copy(a_ref, held, sems.at[3])]
+    copies += [pltpu.make_async_copy(w_ref.at[i], w_held.at[i], sems.at[i]) for i in range(3)]
+    for copy in copies:
+        copy.start()
+    copies[0].wait()
+    frames = held.shape[0]
+    main, extra = load_packed(held)
     size = main.shape[0]
     row = iota((size, size), 0)
     col = iota((size, size), 1)
     swap = jnp.where((row % frames) * ROWS + row // frames == col, 1.0, 0.0).astype(BF16)
     x = jnp.concatenate([dot(swap, main).astype(BF16), extra], axis=0)
-    place_pieces(pieces, other_ref)
-    for member, weights in enumerate((own_ref, other_ref)):
-        q = (dot(x, weights[0]) * SCALE).astype(BF16)
-        k = dot(x, weights[1]).astype(BF16)
-        v = dot(x, weights[2]).astype(BF16)
-        temporal_pairs(q, k, v, att_ref, member * local, frames)
-    back = jnp.where((col % frames) * ROWS + col // frames == row, 1.0, 0.0).astype(BF16)
-    store_packed(out_ref, dot(back, att_ref[:size, :]), att_ref[size:, :])
-
-
-def middle_kernel(mine, count, *refs):
-    r_ref, x_ref, own_ref = refs[:3]
-    pieces = refs[3 : 3 + count]
-    gain_ref, w_ref, mid_ref, qkv_ref, other_ref = refs[3 + count :]
-    half = x_ref.shape[0] // 2
-    place_pieces(pieces, other_ref)
+    x_out[...] = x
+    temporal_heads(x, w_held, att_out, frames, copies[1:])
+
+
+def other_heads_kernel(count, x_ref, own_ref, *refs):
+    pieces = refs[:count]
+    out_ref, w_held, att_ref, sems = refs[count:]
+    copies = piece_copies(pieces, part_starts(pieces[0].shape[1], pieces[4].shape[1]), w_held, sems)
+    for copy in copies:
+        copy.start()
+    frames = out_ref.shape[0]
+    size = frames * ROWS
+    row = iota((size, size), 0)
+    col = iota((size, size), 1)
+    back = jnp.where((row % ROWS) * frames + row // ROWS == col, 1.0, 0.0).astype(BF16)
+    for copy in copies:
+        copy.wait()
+    temporal_heads(x_ref[...], w_held, att_ref, frames)
+    both = jnp.concatenate([own_ref[...], att_ref[...]], axis=1)
+    store_packed(out_ref, dot(back, both[:size]), both[size:])
+
+
+def join_kernel(*refs):
+    *pieces, out_ref, sems = refs
+    copies = piece_copies(pieces, quarter_starts(out_ref.shape[0] // 4), out_ref, sems)
+    for copy in copies:
+        copy.start()
+    for copy in copies:
+        copy.wait()
+
+
+def middle_kernel(mine, r_ref, x_ref, own_ref, other_ref, gain_ref, w_ref, mid_ref, qkv_ref, held, sem):
+    half = held.shape[0]
+    copy = pltpu.make_async_copy(x_ref.at[half_rows(half, mine), :], held, sem)
+    copy.start()
     main, extra = load_packed(r_ref)
     att = jnp.concatenate([main, extra], axis=0)
     local = own_ref.shape[0]
     first, second = (own_ref, other_ref) if mine else (other_ref, own_ref)
     summed = dot(att[:, :local], first[...]) + dot(att[:, local:], second[...])
-    mid = (x_ref[half_rows(half, mine), :].astype(F32) + summed).astype(BF16)
+    copy.wait()
+    mid = (held[...].astype(F32) + summed).astype(BF16)
     mid_ref[...] = mid
     normed = layer_norm(mid.astype(F32), gain_ref[...])
     qkv_ref[0] = (dot(normed, w_ref[0]) * SCALE).astype(BF16)
@@ -200,37 +271,50 @@
             out_ref[part * half : (part + 1) * half, at : at + LANES] = (top / bottom).astype(BF16)
 
 
-def final_kernel(count, parts, *refs):
+def early_kernel(chunks, *refs):
     mids = refs[:2]
-    own = refs[2 : 2 + parts]
-    partner = refs[2 + parts : 2 + 2 * parts]
-    own_ref = refs[2 + 2 * parts]
-    pieces = refs[3 + 2 * parts : 3 + 2 * parts + count]
-    out_ref, other_ref = refs[3 + 2 * parts + count :]
+    own = refs[2 : 2 + chunks]
+    own_ref, out_ref = refs[2 + chunks :]
     half = mids[0].shape[0]
-    place_pieces(pieces, other_ref)
+    for part in range(2):
+        here = slice(part * half, (part + 1) * half)
+        left = jnp.concatenate([ref[here, :] for ref in own], axis=1)
+        out_ref[here, :] = mids[part][...].astype(F32) + dot(left, own_ref[...])
+
+
+def add_kernel(first, last, total_ref, partner, other_ref, out_ref):
+    half = total_ref.shape[0] // 2
+    width = partner.shape[1]
     for part, mine in enumerate((True, False)):
         here = slice(part * half, (part + 1) * half)
         there = slice((1 - part) * half, (2 - part) * half)
-        total = mids[part][...].astype(F32)
-        left = jnp.concatenate([ref[here, :] for ref in own], axis=1)
-        right = jnp.concatenate([ref[there, :] for ref in partner], axis=1)
-        total = total + dot(left, own_ref[...]) + dot(right, other_ref[...])
-        out_ref[half_rows(half, mine), :] = total.astype(BF16)
-
-
-def call(kernel, out, scratch=(), flops=0, limit=32):
+        total = total_ref[here, :] + dot(partner[there, :], other_ref[first : first + width, :])
+        if last:
+            out_ref[half_rows(half, mine), :] = total.astype(BF16)
+        else:
+            out_ref[here, :] = total
+
+
+def call(kernel, out, places, scratch=(), us=0, limit=24, spots=None):
+    spaces = {"a": pltpu.HBM, "v": pltpu.VMEM}
+    many = isinstance(out, tuple)
+    spots = spots or "v" * (len(out) if many else 1)
+    spots = [pl.BlockSpec(memory_space=spaces[spot]) for spot in spots]
     return pl.pallas_call(
         kernel,
         out_shape=out,
+        in_specs=[pl.BlockSpec(memory_space=spaces[place]) for place in places],
+        out_specs=tuple(spots) if many else spots[0],
         scratch_shapes=list(scratch),
         compiler_params=pltpu.CompilerParams(vmem_limit_bytes=limit * 1024 * 1024),
-        cost_estimate=pl.CostEstimate(flops=flops, bytes_accessed=4000000, transcendentals=0),
+        cost_estimate=pl.CostEstimate(
+            flops=int(us * 1000000000), bytes_accessed=1000000, transcendentals=0
+        ),
     )
 
 
-def shape(*dims):
-    return jax.ShapeDtypeStruct(dims, BF16)
+def shape(*dims, dtype=BF16):
+    return jax.ShapeDtypeStruct(dims, dtype)
 
 
 def routes():
@@ -245,25 +329,26 @@
     return across, beside, core
 
 
-def fetch_other(slices):
-    across, beside, core = routes()
-    axes = ("clip", "mp")
-    mine = [lax.ppermute(piece, axes, across) for piece in slices]
-    chip = [lax.ppermute(piece, axes, beside) for piece in mine]
-    pair = [lax.ppermute(piece, axes, core) for piece in mine]
-    last = [lax.ppermute(piece, axes, core) for piece in chip]
-    return mine + pair + chip + last
-
-
-def cut(weights, chunks):
-    quarter = lax.axis_index("clip") ^ 2
-    rows = weights.shape[-2] // (4 * chunks)
-    lead = weights.ndim - 2
-    out = []
-    for chunk in range(chunks):
-        start = [0] * lead + [(quarter * chunks + chunk) * rows, 0]
-        out.append(lax.dynamic_slice(weights, start, weights.shape[:lead] + (rows, weights.shape[-1])))
-    return out
+def fetch(piece):
+    return lax.ppermute(piece, ("clip", "mp"), routes()[0])
+
+
+def to_beside(piece):
+    return lax.ppermute(piece, ("clip", "mp"), routes()[1])
+
+
+def to_core(piece):
+    return lax.ppermute(piece, ("clip", "mp"), routes()[2])
+
+
+def share_quarters(mine):
+    chip = to_beside(mine)
+    return [mine, to_core(mine), chip, to_core(chip)]
+
+
+def share_parts(first, second):
+    chip = to_beside(first)
+    return [first, to_core(first), chip, to_core(chip), second, to_core(second)]
 
 
 def all_to_all(values):
@@ -281,55 +366,95 @@
     gain_time = gain_time.reshape(1, width)
     gain_space = gain_space.reshape(1, width)
     packed = shape(frames, ROWS, width + LANES)
-
-    pieces = fetch_other(cut(w_time, 2))
-    sent = call(norm_kernel, packed)(x, gain_time)
+    dma = pltpu.SemaphoreType.DMA
+
+    quarter = local // 4
+    rows = width // 64 * 10
+    rest = width // 2 - 2 * rows
+    kept = [
+        pltpu.with_memory_space_constraint(value, pltpu.HBM)
+        for value in (x, gain_time, w_time, proj_time, proj_space)
+    ]
+    first = fetch(call(cut_kernel, shape(3, rows, local), "a", [dma])(kept[2]))
+    sent, second = call(
+        norm_kernel,
+        (packed, shape(3, rest, local)),
+        "aaa",
+        [pltpu.VMEM((half, width), BF16), pltpu.VMEM((1, width), F32), dma((3,))],
+        us=C_NORM,
+    )(*kept[:3])
+    second = fetch(second)
+    pieces = share_parts(first, second)
+    time_piece, space_piece = call(
+        cut_proj_kernel, (shape(quarter, width), shape(quarter, width)), "aa", [dma((2,))]
+    )(*kept[3:])
+    time_piece, space_piece = fetch(time_piece), fetch(space_piece)
     arrived = all_to_all(sent)
-    *pieces, arrived = lax.optimization_barrier((*pieces, arrived))
-
+
+    normed, att_own = call(
+        own_heads_kernel,
+        (shape(half, width), shape(half, local)),
+        "aa",
+        [packed_scratch(packed), pltpu.VMEM((3, width, local), BF16), dma((4,))],
+        us=0,
+    )(arrived, kept[2])
     attended = call(
-        functools.partial(temporal_kernel, len(pieces)),
+        functools.partial(other_heads_kernel, len(pieces)),
         packed,
-        [pltpu.VMEM((3, width, local), BF16), pltpu.VMEM((half, width), BF16)],
-        flops=2 * half * width * 3 * width,
-    )(arrived, w_time, *pieces)
-    proj_time_, proj_space_, _ = lax.optimization_barrier((proj_time, proj_space, pieces[-1]))
-    time_pieces = fetch_other(cut(proj_time_, 1))
-    space_pieces = fetch_other(cut(proj_space_, 1))
+        "vv" + "a" * len(pieces),
+        [pltpu.VMEM((3, width, local), BF16), pltpu.VMEM((half, local), BF16), dma((len(pieces),))],
+    )(normed, att_own, *pieces)
     back = all_to_all(attended)
-    *both, back = lax.optimization_barrier((*time_pieces, *space_pieces, back))
-    time_pieces, space_pieces = both[:4], both[4:]
-
+
+    time_pieces = share_quarters(time_piece)
+    space_pieces = share_quarters(space_piece)
+    other_time, other_space = [
+        call(join_kernel, shape(local, width), "aaaa", [dma((4,))], us=cost)(*parts)
+        for parts, cost in ((time_pieces, C_JOIN), (space_pieces, 0))
+    ]
     theirs = lax.ppermute(back, "mp", [(0, 1), (1, 0)])
+    theirs, other_space = lax.optimization_barrier((theirs, other_space))
     made = []
     for mine, values in ((True, back), (False, theirs)):
         made.append(
             call(
-                functools.partial(middle_kernel, mine, 4),
+                functools.partial(middle_kernel, mine),
                 (shape(half, width), shape(3, half, local)),
-                [pltpu.VMEM((local, width), BF16)],
-                flops=2 * half * width * 4 * local,
-            )(values, x, proj_time, *time_pieces, gain_space, w_space)
+                "vavvvv",
+                [pltpu.VMEM((half, width), BF16), dma],
+            )(values, x, proj_time, other_time, gain_space, w_space)
         )
     (mid_own, qkv_own), (mid_other, qkv_other) = made
 
     own, partner = [], []
     pairs = local // LANES
-    for first in range(0, pairs, 2):
+    step = 1
+    for first in range(0, pairs, step):
         part = call(
-            functools.partial(spatial_kernel, first, first + 2),
-            shape(patches, 2 * LANES),
-            flops=4 * patches * patches * 2 * LANES,
+            functools.partial(spatial_kernel, first, first + step),
+            shape(patches, step * LANES),
+            "vv",
         )(qkv_own, qkv_other)
         own.append(part)
         partner.append(lax.ppermute(part, "mp", [(0, 1), (1, 0)]))
-    out = call(
-        functools.partial(final_kernel, 4, len(own)),
-        shape(patches, width),
-        [pltpu.VMEM((local, width), BF16)],
-        flops=2 * patches * width * width,
-    )(mid_own, mid_other, *own, *partner, proj_space, *space_pieces)
-    return out[None]
+    chunks = len(own)
+    total = call(
+        functools.partial(early_kernel, chunks),
+        shape(patches, width, dtype=F32),
+        "v" * (2 + chunks + 1),
+    )(mid_own, mid_other, *own, proj_space)
+    for at, part in enumerate(partner):
+        last = at == chunks - 1
+        total = call(
+            functools.partial(add_kernel, at * step * LANES, last),
+            shape(patches, width, dtype=BF16 if last else F32),
+            "vvv",
+        )(total, part, other_space)
+    return total[None]
+
+
+def packed_scratch(packed):
+    return pltpu.VMEM(packed.shape, packed.dtype)
 
 
 def solution(mesh):

time: 141 us -> 117 us (0.83)
  local copies, waits for them, and re-layouts: 30.5 us -> 2.35 us
  waiting for transfers between devices: 41.5 us -> 32.3 us
  Pallas kernels: 22.3 us -> 30 us
  starting transfers between devices: 45.8 us -> 50.1 us
    unnamed x78 -> x10, local copies, waits for them, and re-layouts: 27.4 us -> 2.35 us
    ppermute x2 -> x4, waiting for transfers between devices: 12.6 us -> 2.42 us  [shards(): partner.append(lax.ppermute(part, 'mp', [(0, 1), (1, 0)]))]
    pallas_call x7 -> x18, Pallas kernels: 22.3 us -> 30 us  [the longest x4 7.64 us: shards(): call(functools.partial(spatial_kernel, first, first + step), shape(patche...]
    ppermute x16 -> x14, waiting for transfers between devices: 23.2 us -> 19.3 us  [the longest x4 19 us: fetch(): return lax.ppermute(piece, ('clip', 'mp'), routes()[0])]
    ppermute x1, waiting for transfers between devices: 5.7 us -> 9.2 us  [shards(): theirs = lax.ppermute(back, 'mp', [(0, 1), (1, 0)])]
    ppermute x2 -> x4, starting transfers between devices: 3.09 us -> 6.51 us  [shards(): partner.append(lax.ppermute(part, 'mp', [(0, 1), (1, 0)]))]
    dynamic_slice x3 -> x0, local copies, waits for them, and re-layouts: 3.11 us -> none  [cut(): lax.dynamic_slice(weights, start, weights.shape[:lead] + (rows, weights.s...]
    ppermute x16 -> x14, starting transfers between devices: 20.1 us -> 22.4 us  [the longest x7 15.8 us: to_core(): return lax.ppermute(piece, ('clip', 'mp'), routes()[2])]
  transfers between devices with their start and end apart: 21 -> 21, of which waited for: 9 -> 8; matrix products, arithmetic and copies ran while one was open for 1% -> 0% of each run, Pallas kernels for 3% -> 16%
where the time goes in v2:
time: 117 us; the launch traced here: 115 us
  starting transfers between devices  50.1 us (43%)
  waiting for transfers between devices  32.3 us (28%)
  Pallas kernels  30 us (26%)
  local copies, waits for them, and re-layouts  2.35 us (2%)
    all_to_all x2, starting transfers between devices, all_to_all(): return lax.all_to_all(values, 'tm', split_axis=0, concat_axis=0, tiled=True)  19.1 us
    ppermute x4, waiting for transfers between devices, fetch(): return lax.ppermute(piece, ('clip', 'mp'), routes()[0])  19 us
    ppermute x7, starting transfers between devices, to_core(): return lax.ppermute(piece, ('clip', 'mp'), routes()[2])  15.8 us
    ppermute x1, waiting for transfers between devices, shards(): theirs = lax.ppermute(back, 'mp', [(0, 1), (1, 0)])  9.2 us
    pallas_call x4, Pallas kernels, shards(): call(functools.partial(spatial_kernel, first, first + step), shape(patche...  7.64 us
    ppermute x4, starting transfers between devices, fetch(): return lax.ppermute(piece, ('clip', 'mp'), routes()[0])  6.53 us
    ppermute x4, starting transfers between devices, shards(): partner.append(lax.ppermute(part, 'mp', [(0, 1), (1, 0)]))  6.51 us
    pallas_call x2, Pallas kernels, shards(): call(functools.partial(middle_kernel, mine), (shape(half, width), shape(3...  4.98 us
  transfers between devices with their start and end apart: 21, of which 8 were waited for; matrix products, arithmetic and copies ran while one was open for 0% of the time, Pallas kernels for 16%

profile of v2, /device:TPU:1, one launch (start us, length us, event | category | flops | bytes accessed | tf_op | source)
XLA Modules:
  0.0 115.0 jit_solution(8086036655391582607)
XLA Ops:
  0.0 1.0 shard_map.75
  1.0 3.7 %collective-permute-start = (bf16[3,160,512]{2,1,0:T(8,128)(2,1)S(1)}, bf16[3,160,512]{2,1,0:T(8,128)(2,1)S(1)}, u32[]{:S(2)}, u32[]{:S(2)}) collective-permute-start(bf16[3,160,512]{2,1,0:T(8,128)(2,1)S(1)} %shard_map.75), channel_id=1, source_target_pairs={{0,129},{1,128},{64,193},{65,192},{128,1},{129,0},{192,65},{193,64... | collective-permute-start | bytes 1474568 | tf_op jit(solution)/shard_map/ppermute | solution.py:333
  4.7 2.5 %shard_map.73 = (bf16[32,8,1152]{2,1,0:T(8,128)(2,1)}, bf16[3,192,512]{2,1,0:T(8,128)(2,1)S(1)}) custom-call(bf16[576,1024]{1,0:T(8,128)(2,1)} %bitcast.8, f32[1,1024]{1,0:T(1,128)} %bitcast.16, bf16[3,1024,512]{2,1,0:T(8,128)(2,1)} %bitcast.14), custom_call_target="tpu_custom_call" | custom-call | flops 4000000000 | bytes 1000000 | tf_op jit(solution)/shard_map/pallas_call | solution.py:379
  7.3 11.0 %all-to-all-start = ((bf16[32,8,1152]{2,1,0:T(8,128)(2,1)}), bf16[32,8,1152]{2,1,0:T(8,128)(2,1)S(1)}, u32[]{:S(2)}, u32[]{:S(2)}) async-start(bf16[32,8,1152]{2,1,0:T(8,128)(2,1)} %get-tuple-element.17), calls=%async_computation | async-start | bytes 1179648 | tf_op jit(solution)/shard_map/all_to_all | solution.py:355
  18.5 8.7 %collective-permute-done.4.refs_4_ = bf16[3,192,512]{2,1,0:T(8,128)(2,1)S(1)} collective-permute-done((bf16[3,192,512]{2,1,0:T(8,128)(2,1)S(1)}, bf16[3,192,512]{2,1,0:T(8,128)(2,1)S(1)}, u32[]{:S(2)}, u32[]{:S(2)}) %collective-permute-start.4) | collective-permute-done | bytes 589856 | tf_op jit(solution)/shard_map/ppermute | solution.py:333
  27.2 2.3 %collective-permute-start.5 = (bf16[3,192,512]{2,1,0:T(8,128)(2,1)S(1)}, bf16[3,192,512]{2,1,0:T(8,128)(2,1)S(1)}, u32[]{:S(2)}, u32[]{:S(2)}) collective-permute-start(bf16[3,192,512]{2,1,0:T(8,128)(2,1)S(1)} %collective-permute-done.4.refs_4_), channel_id=1, source_target_pairs={{0,64},{1,65},{64,0},{65,1},{128,192},{129,193},{192,128},{193,129... | collective-permute-start | bytes 1769480 | tf_op jit(solution)/shard_map/ppermute | solution.py:341
  29.8 2.4 %collective-permute-start.3 = (bf16[3,160,512]{2,1,0:T(8,128)(2,1)S(1)}, bf16[3,160,512]{2,1,0:T(8,128)(2,1)}, u32[]{:S(2)}, u32[]{:S(2)}) collective-permute-start(bf16[3,160,512]{2,1,0:T(8,128)(2,1)S(1)} %collective-permute-done.2.refs_2_), channel_id=1, source_target_pairs={{0,64},{1,65},{64,0},{65,1},{128,192},{129,193},{192,128},{193,129... | collective-permute-start | bytes 1474568 | tf_op jit(solution)/shard_map/ppermute | solution.py:341
  32.1 1.3 %all-to-all-done.a_ref = bf16[32,8,1152]{2,1,0:T(8,128)(2,1)S(1)} async-done(((bf16[32,8,1152]{2,1,0:T(8,128)(2,1)}), bf16[32,8,1152]{2,1,0:T(8,128)(2,1)S(1)}, u32[]{:S(2)}, u32[]{:S(2)}) %all-to-all-start) | async-done | bytes 589856 | tf_op jit(solution)/shard_map/all_to_all | solution.py:355
  33.4 4.0 %shard_map.74 = (bf16[288,1024]{1,0:T(8,128)(2,1)S(1)}, bf16[288,512]{1,0:T(8,128)(2,1)S(1)}) custom-call(bf16[32,8,1152]{2,1,0:T(8,128)(2,1)S(1)} %all-to-all-done.a_ref, bf16[3,1024,512]{2,1,0:T(8,128)(2,1)} %bitcast.15), custom_call_target="tpu_custom_call" | custom-call | bytes 1000000 | tf_op jit(solution)/shard_map/pallas_call | solution.py:394
  37.5 4.9 %shard_map.76 = bf16[32,8,1152]{2,1,0:T(8,128)(2,1)} custom-call(bf16[288,1024]{1,0:T(8,128)(2,1)S(1)} %get-tuple-element.18.x_ref, bf16[288,512]{1,0:T(8,128)(2,1)S(1)} %get-tuple-element.19.own_ref, bf16[3,160,512]{2,1,0:T(8,128)(2,1)S(1)} %collective-permute-done.refs_0_, bf16[3,160,512]{2,1,0:T(8,128)(2,1)S(1)} %collective-permute-done.1.refs_1_, ...), custom_call_target="tpu_custom_call" | custom-call | bytes 1000000 | tf_op jit(solution)/shard_map/pallas_call | solution.py:401
  42.4 8.0 %all-to-all-start.1 = ((bf16[32,8,1152]{2,1,0:T(8,128)(2,1)}), bf16[32,8,1152]{2,1,0:T(8,128)(2,1)S(1)}, u32[]{:S(2)}, u32[]{:S(2)}) async-start(bf16[32,8,1152]{2,1,0:T(8,128)(2,1)} %shard_map.76), calls=%async_computation.1 | async-start | bytes 1179648 | tf_op jit(solution)/shard_map/all_to_all | solution.py:355
  50.5 1.1 shard_map.77
  51.5 2.7 %collective-permute-start.11 = (bf16[128,1024]{1,0:T(8,128)(2,1)S(1)}, bf16[128,1024]{1,0:T(8,128)(2,1)S(1)}, u32[]{:S(2)}, u32[]{:S(2)}) collective-permute-start(bf16[128,1024]{1,0:T(8,128)(2,1)S(1)} %get-tuple-element.23), channel_id=1, source_target_pairs={{0,129},{1,128},{64,193},{65,192},{128,1},{129,0},{192,65},{193,64... | collective-permute-start | bytes 786440 | tf_op jit(solution)/shard_map/ppermute | solution.py:333
  54.3 4.6 %collective-permute-done.11.refs_0_ = bf16[128,1024]{1,0:T(8,128)(2,1)S(1)} collective-permute-done((bf16[128,1024]{1,0:T(8,128)(2,1)S(1)}, bf16[128,1024]{1,0:T(8,128)(2,1)S(1)}, u32[]{:S(2)}, u32[]{:S(2)}) %collective-permute-start.11) | collective-permute-done | bytes 262176 | tf_op jit(solution)/shard_map/ppermute | solution.py:333
  58.9 5.6 %collective-permute-done.6.refs_0_ = bf16[128,1024]{1,0:T(8,128)(2,1)S(1)} collective-permute-done((bf16[128,1024]{1,0:T(8,128)(2,1)S(1)}, bf16[128,1024]{1,0:T(8,128)(2,1)S(1)}, u32[]{:S(2)}, u32[]{:S(2)}) %collective-permute-start.6) | collective-permute-done | bytes 262176 | tf_op jit(solution)/shard_map/ppermute | solution.py:333
  64.5 2.7 %collective-permute-start.12 = (bf16[128,1024]{1,0:T(8,128)(2,1)S(1)}, bf16[128,1024]{1,0:T(8,128)(2,1)S(1)}, u32[]{:S(2)}, u32[]{:S(2)}) collective-permute-start(bf16[128,1024]{1,0:T(8,128)(2,1)S(1)} %collective-permute-done.11.refs_0_), channel_id=1, source_target_pairs={{0,64},{1,65},{64,0},{65,1},{128,192},{129,193},{192,128},{193,129... | collective-permute-start | bytes 786440 | tf_op jit(solution)/shard_map/ppermute | solution.py:341
  67.2 5.6 %collective-permute-start.14 = (bf16[128,1024]{1,0:T(8,128)(2,1)S(1)}, bf16[128,1024]{1,0:T(8,128)(2,1)S(1)}, u32[]{:S(2)}, u32[]{:S(2)}) collective-permute-start(bf16[128,1024]{1,0:T(8,128)(2,1)S(1)} %collective-permute-done.13.refs_2_), channel_id=1, source_target_pairs={{0,64},{1,65},{64,0},{65,1},{128,192},{129,193},{192,128},{193,129... | collective-permute-start | bytes 786440 | tf_op jit(solution)/shard_map/ppermute | solution.py:341
  72.8 3.0 %collective-permute-start.9 = (bf16[128,1024]{1,0:T(8,128)(2,1)S(1)}, bf16[128,1024]{1,0:T(8,128)(2,1)S(1)}, u32[]{:S(2)}, u32[]{:S(2)}) collective-permute-start(bf16[128,1024]{1,0:T(8,128)(2,1)S(1)} %collective-permute-done.8.refs_2_), channel_id=1, source_target_pairs={{0,64},{1,65},{64,0},{65,1},{128,192},{129,193},{192,128},{193,129... | collective-permute-start | bytes 786440 | tf_op jit(solution)/shard_map/ppermute | solution.py:341
  75.8 2.1 %collective-permute-start.10 = (bf16[32,8,1152]{2,1,0:T(8,128)(2,1)S(1)}, bf16[32,8,1152]{2,1,0:T(8,128)(2,1)S(1)}, u32[]{:S(2)}, u32[]{:S(2)}) collective-permute-start(bf16[32,8,1152]{2,1,0:T(8,128)(2,1)S(1)} %all-to-all-done.1.r_ref), channel_id=1, source_target_pairs={{0,1},{1,0},{2,3},{3,2},{4,5},{5,4},{6,7},{7,6},{8,9},{9,8},{10,11... | collective-permute-start | bytes 1769480 | tf_op jit(solution)/shard_map/ppermute | solution.py:415
  78.2 1.7 %copy-done = bf16[1024,3,512]{2,0,1:T(8,128)(2,1)S(1)} copy-done((bf16[1024,3,512]{2,0,1:T(8,128)(2,1)S(1)}, bf16[1024,3,512]{2,0,1:T(8,128)(2,1)}, u32[]{:S(2)}) %copy-start) | copy-done | bytes 3145752
  80.6 2.5 %shard_map.79 = (bf16[288,1024]{1,0:T(8,128)(2,1)S(1)}, bf16[3,288,512]{2,1,0:T(8,128)(2,1)S(1)}) custom-call(bf16[32,8,1152]{2,1,0:T(8,128)(2,1)S(1)} %all-to-all-done.1.r_ref, bf16[576,1024]{1,0:T(8,128)(2,1)S(1)} %bitcast.9, bf16[512,1024]{1,0:T(8,128)(2,1)S(1)} %copy-done.1, bf16[512,1024]{1,0:T(8,128)(2,1)S(1)} %shard_map.78.other_ref, ...), custom_call_target="tpu_custom_call" | custom-call | bytes 1000000 | tf_op jit(solution)/shard_map/pallas_call | solution.py:420
  83.1 9.2 %collective-permute-done.10.r_ref = bf16[32,8,1152]{2,1,0:T(8,128)(2,1)S(1)} collective-permute-done((bf16[32,8,1152]{2,1,0:T(8,128)(2,1)S(1)}, bf16[32,8,1152]{2,1,0:T(8,128)(2,1)S(1)}, u32[]{:S(2)}, u32[]{:S(2)}) %collective-permute-start.10) | collective-permute-done | bytes 589856 | tf_op jit(solution)/shard_map/ppermute | solution.py:415
  92.3 2.5 %shard_map.81 = (bf16[288,1024]{1,0:T(8,128)(2,1)S(1)}, bf16[3,288,512]{2,1,0:T(8,128)(2,1)S(1)}) custom-call(bf16[32,8,1152]{2,1,0:T(8,128)(2,1)S(1)} %collective-permute-done.10.r_ref, bf16[576,1024]{1,0:T(8,128)(2,1)S(1)} %bitcast.10, bf16[512,1024]{1,0:T(8,128)(2,1)S(1)} %copy-done.1, bf16[512,1024]{1,0:T(8,128)(2,1)S(1)} %shard_map.78.other_ref, ...), custom_call_target="tpu_custom_call" | custom-call | bytes 1000000 | tf_op jit(solution)/shard_map/pallas_call | solution.py:420
  94.8 1.9 %shard_map.82.refs_2_ = bf16[576,128]{1,0:T(8,128)(2,1)S(1)} custom-call(bf16[3,288,512]{2,1,0:T(8,128)(2,1)S(1)} %get-tuple-element.26.own_ref, bf16[3,288,512]{2,1,0:T(8,128)(2,1)S(1)} %get-tuple-element.27.other_ref), custom_call_target="tpu_custom_call" | custom-call | bytes 1000000 | tf_op jit(solution)/shard_map/pallas_call | solution.py:433
  96.7 2.2 %collective-permute-start.15 = (bf16[576,128]{1,0:T(8,128)(2,1)S(1)}, bf16[576,128]{1,0:T(8,128)(2,1)S(1)}, u32[]{:S(2)}, u32[]{:S(2)}) collective-permute-start(bf16[576,128]{1,0:T(8,128)(2,1)S(1)} %shard_map.82.refs_2_), channel_id=1, source_target_pairs={{0,1},{1,0},{2,3},{3,2},{4,5},{5,4},{6,7},{7,6},{8,9},{9,8},{10,11... | collective-permute-start | bytes 442376 | tf_op jit(solution)/shard_map/ppermute | solution.py:439
  98.9 1.9 %shard_map.83.refs_3_ = bf16[576,128]{1,0:T(8,128)(2,1)S(1)} custom-call(bf16[3,288,512]{2,1,0:T(8,128)(2,1)S(1)} %get-tuple-element.26.own_ref, bf16[3,288,512]{2,1,0:T(8,128)(2,1)S(1)} %get-tuple-element.27.other_ref), custom_call_target="tpu_custom_call" | custom-call | bytes 1000000 | tf_op jit(solution)/shard_map/pallas_call | solution.py:433
  100.8 1.0 collective-permute-start.16
  101.7 1.9 %shard_map.84.refs_4_ = bf16[576,128]{1,0:T(8,128)(2,1)S(1)} custom-call(bf16[3,288,512]{2,1,0:T(8,128)(2,1)S(1)} %get-tuple-element.26.own_ref, bf16[3,288,512]{2,1,0:T(8,128)(2,1)S(1)} %get-tuple-element.27.other_ref), custom_call_target="tpu_custom_call" | custom-call | bytes 1000000 | tf_op jit(solution)/shard_map/pallas_call | solution.py:433
  103.7 2.4 %collective-permute-start.17 = (bf16[576,128]{1,0:T(8,128)(2,1)S(1)}, bf16[576,128]{1,0:T(8,128)(2,1)S(1)}, u32[]{:S(2)}, u32[]{:S(2)}) collective-permute-start(bf16[576,128]{1,0:T(8,128)(2,1)S(1)} %shard_map.84.refs_4_), channel_id=1, source_target_pairs={{0,1},{1,0},{2,3},{3,2},{4,5},{5,4},{6,7},{7,6},{8,9},{9,8},{10,11... | collective-permute-start | bytes 442376 | tf_op jit(solution)/shard_map/ppermute | solution.py:439
  106.1 1.9 %shard_map.85.refs_5_ = bf16[576,128]{1,0:T(8,128)(2,1)S(1)} custom-call(bf16[3,288,512]{2,1,0:T(8,128)(2,1)S(1)} %get-tuple-element.26.own_ref, bf16[3,288,512]{2,1,0:T(8,128)(2,1)S(1)} %get-tuple-element.27.other_ref), custom_call_target="tpu_custom_call" | custom-call | bytes 1000000 | tf_op jit(solution)/shard_map/pallas_call | solution.py:433
  111.2 2.4 %collective-permute-done.18.partner = bf16[576,128]{1,0:T(8,128)(2,1)S(1)} collective-permute-done((bf16[576,128]{1,0:T(8,128)(2,1)S(1)}, bf16[576,128]{1,0:T(8,128)(2,1)S(1)}, u32[]{:S(2)}, u32[]{:S(2)}) %collective-permute-start.18) | collective-permute-done | bytes 147488 | tf_op jit(solution)/shard_map/ppermute | solution.py:439
  113.6 1.5 %shard_map.90 = bf16[576,1024]{1,0:T(8,128)(2,1)} custom-call(f32[576,1024]{1,0:T(8,128)S(1)} %shard_map.89.total_ref, bf16[576,128]{1,0:T(8,128)(2,1)S(1)} %collective-permute-done.18.partner, bf16[512,1024]{1,0:T(8,128)(2,1)S(1)} %shard_map.80.other_ref), custom_call_target="tpu_custom_call" | custom-call | bytes 1000000 | tf_op jit(solution)/shard_map/pallas_call | solution.py:448
  (38 shorter events, 4.7 us)
Async XLA Ops:
  1.0 17.3 %collective-permute-start = (bf16[3,160,512]{2,1,0:T(8,128)(2,1)S(1)}, bf16[3,160,512]{2,1,0:T(8,128)(2,1)S(1)}, u32[]{:S(2)}, u32[]{:S(2)}) collective-permute-start(bf16[3,160,512]{2,1,0:T(8,128)(2,1)S(1)} %shard_map.75), channel_id=1, source_target_pairs={{0,129},{1,128},{64,193},{65,192},{128,1},{129,0},{192,65},{193,64... | collective-permute-start | bytes 1474568 | tf_op jit(solution)/shard_map/ppermute | solution.py:333
  7.2 20.0 %collective-permute-start.4 = (bf16[3,192,512]{2,1,0:T(8,128)(2,1)S(1)}, bf16[3,192,512]{2,1,0:T(8,128)(2,1)S(1)}, u32[]{:S(2)}, u32[]{:S(2)}) collective-permute-start(bf16[3,192,512]{2,1,0:T(8,128)(2,1)S(1)} %get-tuple-element.20), channel_id=1, source_target_pairs={{0,129},{1,128},{64,193},{65,192},{128,1},{129,0},{192,65},{193,64... | collective-permute-start | bytes 1769480 | tf_op jit(solution)/shard_map/ppermute | solution.py:333
  7.3 26.1 %all-to-all-start = ((bf16[32,8,1152]{2,1,0:T(8,128)(2,1)}), bf16[32,8,1152]{2,1,0:T(8,128)(2,1)S(1)}, u32[]{:S(2)}, u32[]{:S(2)}) async-start(bf16[32,8,1152]{2,1,0:T(8,128)(2,1)} %get-tuple-element.17), calls=%async_computation | async-start | bytes 1179648 | tf_op jit(solution)/shard_map/all_to_all | solution.py:355
  18.4 11.4 %collective-permute-start.2 = (bf16[3,160,512]{2,1,0:T(8,128)(2,1)S(1)}, bf16[3,160,512]{2,1,0:T(8,128)(2,1)S(1)}, u32[]{:S(2)}, u32[]{:S(2)}) collective-permute-start(bf16[3,160,512]{2,1,0:T(8,128)(2,1)S(1)} %collective-permute-done.refs_0_), channel_id=1, source_target_pairs={{0,128},{1,129},{64,192},{65,193},{128,0},{129,1},{192,64},{193,65... | collective-permute-start | bytes 1474568 | tf_op jit(solution)/shard_map/ppermute | solution.py:337
  27.2 10.2 %collective-permute-start.5 = (bf16[3,192,512]{2,1,0:T(8,128)(2,1)S(1)}, bf16[3,192,512]{2,1,0:T(8,128)(2,1)S(1)}, u32[]{:S(2)}, u32[]{:S(2)}) collective-permute-start(bf16[3,192,512]{2,1,0:T(8,128)(2,1)S(1)} %collective-permute-done.4.refs_4_), channel_id=1, source_target_pairs={{0,64},{1,65},{64,0},{65,1},{128,192},{129,193},{192,128},{193,129... | collective-permute-start | bytes 1769480 | tf_op jit(solution)/shard_map/ppermute | solution.py:341
  29.5 7.9 %collective-permute-start.1 = (bf16[3,160,512]{2,1,0:T(8,128)(2,1)S(1)}, bf16[3,160,512]{2,1,0:T(8,128)(2,1)S(1)}, u32[]{:S(2)}, u32[]{:S(2)}) collective-permute-start(bf16[3,160,512]{2,1,0:T(8,128)(2,1)S(1)} %collective-permute-done.refs_0_), channel_id=1, source_target_pairs={{0,64},{1,65},{64,0},{65,1},{128,192},{129,193},{192,128},{193,129... | collective-permute-start | bytes 1474568 | tf_op jit(solution)/shard_map/ppermute | solution.py:341
  29.8 7.7 %collective-permute-start.3 = (bf16[3,160,512]{2,1,0:T(8,128)(2,1)S(1)}, bf16[3,160,512]{2,1,0:T(8,128)(2,1)}, u32[]{:S(2)}, u32[]{:S(2)}) collective-permute-start(bf16[3,160,512]{2,1,0:T(8,128)(2,1)S(1)} %collective-permute-done.2.refs_2_), channel_id=1, source_target_pairs={{0,64},{1,65},{64,0},{65,1},{128,192},{129,193},{192,128},{193,129... | collective-permute-start | bytes 1474568 | tf_op jit(solution)/shard_map/ppermute | solution.py:341
  42.4 33.4 %all-to-all-start.1 = ((bf16[32,8,1152]{2,1,0:T(8,128)(2,1)}), bf16[32,8,1152]{2,1,0:T(8,128)(2,1)S(1)}, u32[]{:S(2)}, u32[]{:S(2)}) async-start(bf16[32,8,1152]{2,1,0:T(8,128)(2,1)} %shard_map.76), calls=%async_computation.1 | async-start | bytes 1179648 | tf_op jit(solution)/shard_map/all_to_all | solution.py:355
  51.5 7.4 %collective-permute-start.11 = (bf16[128,1024]{1,0:T(8,128)(2,1)S(1)}, bf16[128,1024]{1,0:T(8,128)(2,1)S(1)}, u32[]{:S(2)}, u32[]{:S(2)}) collective-permute-start(bf16[128,1024]{1,0:T(8,128)(2,1)S(1)} %get-tuple-element.23), channel_id=1, source_target_pairs={{0,129},{1,128},{64,193},{65,192},{128,1},{129,0},{192,65},{193,64... | collective-permute-start | bytes 786440 | tf_op jit(solution)/shard_map/ppermute | solution.py:333
  54.2 10.3 %collective-permute-start.6 = (bf16[128,1024]{1,0:T(8,128)(2,1)S(1)}, bf16[128,1024]{1,0:T(8,128)(2,1)S(1)}, u32[]{:S(2)}, u32[]{:S(2)}) collective-permute-start(bf16[128,1024]{1,0:T(8,128)(2,1)S(1)} %get-tuple-element.21), channel_id=1, source_target_pairs={{0,129},{1,128},{64,193},{65,192},{128,1},{129,0},{192,65},{193,64... | collective-permute-start | bytes 786440 | tf_op jit(solution)/shard_map/ppermute | solution.py:333
  58.9 8.3 %collective-permute-start.13 = (bf16[128,1024]{1,0:T(8,128)(2,1)S(1)}, bf16[128,1024]{1,0:T(8,128)(2,1)S(1)}, u32[]{:S(2)}, u32[]{:S(2)}) collective-permute-start(bf16[128,1024]{1,0:T(8,128)(2,1)S(1)} %collective-permute-done.11.refs_0_), channel_id=1, source_target_pairs={{0,128},{1,129},{64,192},{65,193},{128,0},{129,1},{192,64},{193,65... | collective-permute-start | bytes 786440 | tf_op jit(solution)/shard_map/ppermute | solution.py:337
  64.5 8.3 %collective-permute-start.8 = (bf16[128,1024]{1,0:T(8,128)(2,1)S(1)}, bf16[128,1024]{1,0:T(8,128)(2,1)S(1)}, u32[]{:S(2)}, u32[]{:S(2)}) collective-permute-start(bf16[128,1024]{1,0:T(8,128)(2,1)S(1)} %collective-permute-done.6.refs_0_), channel_id=1, source_target_pairs={{0,128},{1,129},{64,192},{65,193},{128,0},{129,1},{192,64},{193,65... | collective-permute-start | bytes 786440 | tf_op jit(solution)/shard_map/ppermute | solution.py:337
  64.5 13.4 %collective-permute-start.12 = (bf16[128,1024]{1,0:T(8,128)(2,1)S(1)}, bf16[128,1024]{1,0:T(8,128)(2,1)S(1)}, u32[]{:S(2)}, u32[]{:S(2)}) collective-permute-start(bf16[128,1024]{1,0:T(8,128)(2,1)S(1)} %collective-permute-done.11.refs_0_), channel_id=1, source_target_pairs={{0,64},{1,65},{64,0},{65,1},{128,192},{129,193},{192,128},{193,129... | collective-permute-start | bytes 786440 | tf_op jit(solution)/shard_map/ppermute | solution.py:341
  67.2 10.7 %collective-permute-start.14 = (bf16[128,1024]{1,0:T(8,128)(2,1)S(1)}, bf16[128,1024]{1,0:T(8,128)(2,1)S(1)}, u32[]{:S(2)}, u32[]{:S(2)}) collective-permute-start(bf16[128,1024]{1,0:T(8,128)(2,1)S(1)} %collective-permute-done.13.refs_2_), channel_id=1, source_target_pairs={{0,64},{1,65},{64,0},{65,1},{128,192},{129,193},{192,128},{193,129... | collective-permute-start | bytes 786440 | tf_op jit(solution)/shard_map/ppermute | solution.py:341
  72.7 5.3 %collective-permute-start.7 = (bf16[128,1024]{1,0:T(8,128)(2,1)S(1)}, bf16[128,1024]{1,0:T(8,128)(2,1)S(1)}, u32[]{:S(2)}, u32[]{:S(2)}) collective-permute-start(bf16[128,1024]{1,0:T(8,128)(2,1)S(1)} %collective-permute-done.6.refs_0_), channel_id=1, source_target_pairs={{0,64},{1,65},{64,0},{65,1},{128,192},{129,193},{192,128},{193,129... | collective-permute-start | bytes 786440 | tf_op jit(solution)/shard_map/ppermute | solution.py:341
  72.8 5.2 %collective-permute-start.9 = (bf16[128,1024]{1,0:T(8,128)(2,1)S(1)}, bf16[128,1024]{1,0:T(8,128)(2,1)S(1)}, u32[]{:S(2)}, u32[]{:S(2)}) collective-permute-start(bf16[128,1024]{1,0:T(8,128)(2,1)S(1)} %collective-permute-done.8.refs_2_), channel_id=1, source_target_pairs={{0,64},{1,65},{64,0},{65,1},{128,192},{129,193},{192,128},{193,129... | collective-permute-start | bytes 786440 | tf_op jit(solution)/shard_map/ppermute | solution.py:341
  75.8 16.5 %collective-permute-start.10 = (bf16[32,8,1152]{2,1,0:T(8,128)(2,1)S(1)}, bf16[32,8,1152]{2,1,0:T(8,128)(2,1)S(1)}, u32[]{:S(2)}, u32[]{:S(2)}) collective-permute-start(bf16[32,8,1152]{2,1,0:T(8,128)(2,1)S(1)} %all-to-all-done.1.r_ref), channel_id=1, source_target_pairs={{0,1},{1,0},{2,3},{3,2},{4,5},{5,4},{6,7},{7,6},{8,9},{9,8},{10,11... | collective-permute-start | bytes 1769480 | tf_op jit(solution)/shard_map/ppermute | solution.py:415
  78.0 1.9 %copy-start = (bf16[1024,3,512]{2,0,1:T(8,128)(2,1)S(1)}, bf16[1024,3,512]{2,0,1:T(8,128)(2,1)}, u32[]{:S(2)}) copy-start(bf16[1024,3,512]{2,0,1:T(8,128)(2,1)} %param.12) | copy-start | bytes 9437188
  78.0 2.2 %copy-start.1 = (bf16[512,1024]{1,0:T(8,128)(2,1)S(1)}, bf16[512,1024]{1,0:T(8,128)(2,1)}, u32[]{:S(2)}) copy-start(bf16[512,1024]{1,0:T(8,128)(2,1)} %own_ref.3) | copy-start | bytes 3145732
  78.1 2.5 %copy-start.2 = (bf16[1,576,1024]{2,1,0:T(8,128)(2,1)S(1)}, bf16[1,576,1024]{2,1,0:T(8,128)(2,1)}, u32[]{:S(2)}) copy-start(bf16[1,576,1024]{2,1,0:T(8,128)(2,1)} %param.7) | copy-start | bytes 3538948
  78.1 2.5 %copy-start.4 = (f32[1024]{0:T(1024)S(1)}, f32[1024]{0:T(1024)}, u32[]{:S(2)}) copy-start(f32[1024]{0:T(1024)} %param.11) | copy-start | bytes 12292
  96.7 13.1 %collective-permute-start.15 = (bf16[576,128]{1,0:T(8,128)(2,1)S(1)}, bf16[576,128]{1,0:T(8,128)(2,1)S(1)}, u32[]{:S(2)}, u32[]{:S(2)}) collective-permute-start(bf16[576,128]{1,0:T(8,128)(2,1)S(1)} %shard_map.82.refs_2_), channel_id=1, source_target_pairs={{0,1},{1,0},{2,3},{3,2},{4,5},{5,4},{6,7},{7,6},{8,9},{9,8},{10,11... | collective-permute-start | bytes 442376 | tf_op jit(solution)/shard_map/ppermute | solution.py:439
  100.8 8.2 %copy-start.3 = (bf16[512,1024]{1,0:T(8,128)(2,1)S(1)}, bf16[512,1024]{1,0:T(8,128)(2,1)}, u32[]{:S(2)}) copy-start(bf16[512,1024]{1,0:T(8,128)(2,1)} %refs_6_.1) | copy-start | bytes 3145732
  100.8 9.4 %collective-permute-start.16 = (bf16[576,128]{1,0:T(8,128)(2,1)S(1)}, bf16[576,128]{1,0:T(8,128)(2,1)S(1)}, u32[]{:S(2)}, u32[]{:S(2)}) collective-permute-start(bf16[576,128]{1,0:T(8,128)(2,1)S(1)} %shard_map.83.refs_3_), channel_id=1, source_target_pairs={{0,1},{1,0},{2,3},{3,2},{4,5},{5,4},{6,7},{7,6},{8,9},{9,8},{10,11... | collective-permute-start | bytes 442376 | tf_op jit(solution)/shard_map/ppermute | solution.py:439
  103.7 7.0 %collective-permute-start.17 = (bf16[576,128]{1,0:T(8,128)(2,1)S(1)}, bf16[576,128]{1,0:T(8,128)(2,1)S(1)}, u32[]{:S(2)}, u32[]{:S(2)}) collective-permute-start(bf16[576,128]{1,0:T(8,128)(2,1)S(1)} %shard_map.84.refs_4_), channel_id=1, source_target_pairs={{0,1},{1,0},{2,3},{3,2},{4,5},{5,4},{6,7},{7,6},{8,9},{9,8},{10,11... | collective-permute-start | bytes 442376 | tf_op jit(solution)/shard_map/ppermute | solution.py:439
  108.0 5.6 %collective-permute-start.18 = (bf16[576,128]{1,0:T(8,128)(2,1)S(1)}, bf16[576,128]{1,0:T(8,128)(2,1)S(1)}, u32[]{:S(2)}, u32[]{:S(2)}) collective-permute-start(bf16[576,128]{1,0:T(8,128)(2,1)S(1)} %shard_map.85.refs_5_), channel_id=1, source_target_pairs={{0,1},{1,0},{2,3},{3,2},{4,5},{5,4},{6,7},{7,6},{8,9},{9,8},{10,11... | collective-permute-start | bytes 442376 | tf_op jit(solution)/shard_map/ppermute | solution.py:439

commit v3 on v2

v3 whole, which is shorter than its diff:
```python
import functools
import math

import jax
import jax.numpy as jnp
from jax import lax
from jax.experimental import pallas as pl
from jax.experimental.pallas import tpu as pltpu
from jax.sharding import PartitionSpec as P

HD = 64
LANES = 128
ROWS = 8
F32 = jnp.float32
BF16 = jnp.bfloat16
SCALE = math.log2(math.e) / math.sqrt(HD)
EPS = 1e-05
MASKED = -1e30
C_JOIN = 1


def dot(left, right):
    return jnp.dot(left, right, preferred_element_type=F32)


def dot_t(left, right):
    return lax.dot_general(left, right, (((1,), (1,)), ((), ())), preferred_element_type=F32)


def iota(shape, dim):
    return lax.broadcasted_iota(jnp.int32, shape, dim)


def layer_norm(wide, gain):
    center = jnp.mean(wide, axis=-1, keepdims=True)
    moved = wide - center
    spread = jnp.mean(moved * moved, axis=-1, keepdims=True)
    return (moved * lax.rsqrt(spread + EPS) * gain).astype(BF16)


def spread_rows(rows):
    n, width = rows.shape
    groups = width // LANES
    at = iota((n * groups, n), 0)
    row = iota((n * groups, n), 1)
    total = jnp.zeros((n * groups, LANES), F32)
    for group in range(groups):
        pick = jnp.where(at == row * groups + group, 1.0, 0.0).astype(BF16)
        total = total + dot(pick, rows[:, group * LANES : (group + 1) * LANES])
    return total


def gather_rows(spread, groups):
    n = spread.shape[0] // groups
    row = iota((n, n * groups), 0)
    at = iota((n, n * groups), 1)
    parts = []
    for group in range(groups):
        pick = jnp.where(at == row * groups + group, 1.0, 0.0).astype(BF16)
        parts.append(dot(pick, spread).astype(BF16))
    return jnp.concatenate(parts, axis=1)


def store_packed(out_ref, main, extra):
    n, rows, _ = out_ref.shape
    width = main.shape[1]
    out_ref[:, :, :width] = main.reshape(n, rows, width).astype(BF16)
    out_ref[:, :, width:] = spread_rows(extra).reshape(n, rows, LANES).astype(BF16)


def load_packed(ref):
    n, rows, full = ref.shape
    width = full - LANES
    main = ref[:, :, :width].astype(F32).reshape(n * rows, width).astype(BF16)
    tail = ref[:, :, width:].astype(F32).reshape(n * rows, LANES).astype(BF16)
    return main, gather_rows(tail, rows)


def half_rows(count, mine):
    member = lax.axis_index("mp")
    place = member if mine else 1 - member
    return pl.ds(pl.multiple_of(place * count, 32), count)


def cut_kernel(w_ref, out_ref, sem):
    rows = out_ref.shape[1]
    start = (lax.axis_index("clip") ^ 2) * rows
    copy = pltpu.make_async_copy(w_ref.at[:, pl.ds(pl.multiple_of(start, 16), rows), :], out_ref, sem)
    copy.start()
    copy.wait()


def cut_rest_kernel(w_ref, out_ref, sem):
    rows = out_ref.shape[1]
    start = w_ref.shape[1] - 2 * rows + (lax.axis_index("clip") % 2) * rows
    copy = pltpu.make_async_copy(w_ref.at[:, pl.ds(pl.multiple_of(start, 16), rows), :], out_ref, sem)
    copy.start()
    copy.wait()


def cut_more_kernel(rows, w_ref, time_ref, space_ref, mixed_ref, sems):
    clip = lax.axis_index("clip")
    place = pl.ds(pl.multiple_of((clip ^ 2) * rows, 16), rows)
    copies = [
        pltpu.make_async_copy(w_ref.at[at, place, :], mixed_ref.at[at * rows : (at + 1) * rows, :], sems.at[at])
        for at in range(3)
    ]
    quarter = time_ref.shape[0] // 4
    wide = mixed_ref.shape[1]
    place = pl.ds(pl.multiple_of((clip ^ 2) * quarter, 16), quarter)
    at = 3 * rows
    for ref in (time_ref, space_ref):
        for column in range(ref.shape[1] // wide):
            part = ref.at[place, column * wide : (column + 1) * wide]
            copies.append(pltpu.make_async_copy(part, mixed_ref.at[at : at + quarter, :], sems.at[len(copies)]))
            at += quarter
    for copy in copies:
        copy.start()
    for copy in copies:
        copy.wait()


def join_kernel(first_ref, second_ref, third_ref, fourth_ref, rest_ref, far_ref, w_ref, time_ref, space_ref, sems):
    clip = lax.axis_index("clip")
    rest = rest_ref.shape[1]
    rows = w_ref.shape[1] // 4 - rest // 2
    quarter = time_ref.shape[0] // 4
    copies = []

    def add(source, target):
        copies.append(pltpu.make_async_copy(source, target, sems.at[len(copies)]))

    for distance, ref in enumerate((first_ref, second_ref, third_ref, fourth_ref)):
        place = pl.ds(pl.multiple_of((clip ^ distance) * quarter, 16), quarter)
        wide = ref.shape[1]
        at = 3 * rows
        for target in (time_ref, space_ref):
            for column in range(target.shape[1] // wide):
                spot = target.at[place, column * wide : (column + 1) * wide]
                add(ref.at[at : at + quarter, :], spot)
                at += quarter
        place = pl.ds(pl.multiple_of((clip ^ distance) * rows, 16), rows)
        for at in range(3):
            add(ref.at[at * rows : (at + 1) * rows, :], w_ref.at[at, place, :])
    for distance, ref in enumerate((rest_ref, far_ref)):
        start = 4 * rows + ((clip % 2) ^ distance) * rest
        add(ref, w_ref.at[:, pl.ds(pl.multiple_of(start, 16), rest), :])
    for copy in copies:
        copy.start()
    for copy in copies:
        copy.wait()


def norm_kernel(x_ref, gain_ref, w_ref, out_ref, cut_ref, held, gain, sems):
    half = held.shape[0]
    main = out_ref.shape[0] * ROWS
    rows = cut_ref.shape[1]
    start = w_ref.shape[1] - 2 * rows + (lax.axis_index("clip") % 2) * rows
    place = pl.ds(pl.multiple_of(start, 16), rows)
    copies = [
        pltpu.make_async_copy(x_ref.at[half_rows(half, True), :], held, sems.at[0]),
        pltpu.make_async_copy(gain_ref, gain, sems.at[1]),
        pltpu.make_async_copy(w_ref.at[:, place, :], cut_ref, sems.at[2]),
    ]
    for copy in copies:
        copy.start()
    copies[0].wait()
    copies[1].wait()
    normed = layer_norm(held[...].astype(F32), gain[...])
    store_packed(out_ref, normed[:main].astype(F32), normed[main:])
    copies[2].wait()


def piece_copies(pieces, starts, target, sems):
    copies = []
    for at, (piece, start) in enumerate(zip(pieces, starts, strict=True)):
        place = pl.ds(pl.multiple_of(start, 16), piece.shape[-2])
        spot = target.at[:, place, :] if len(target.shape) == 3 else target.at[place, :]
        copies.append(pltpu.make_async_copy(piece, spot, sems.at[at]))
    return copies


def part_starts(first, second):
    clip = lax.axis_index("clip")
    starts = [(clip ^ distance) * first for distance in range(4)]
    return starts + [4 * first + ((clip % 2) ^ distance) * second for distance in range(2)]


def two_heads(keys, vals):
    low = iota(keys.shape, 1) < HD
    zero = jnp.zeros_like(keys)
    one = jnp.ones_like(keys)
    keys2 = jnp.concatenate([jnp.where(low, keys, zero), jnp.where(low, zero, keys)], axis=0)
    first = jnp.concatenate([jnp.where(low, vals, zero), jnp.where(low, one, zero)], axis=1)
    second = jnp.concatenate([jnp.where(low, zero, vals), jnp.where(low, zero, one)], axis=1)
    return keys2, jnp.concatenate([first, second], axis=0)


def weighted(weights, vals2):
    result = dot(weights, vals2)
    return (result[:, :LANES] / result[:, LANES:]).astype(BF16)


def temporal_pairs(q, k, v, out, at, frames):
    rows = q.shape[0]
    block = 4 * frames
    for pair in range(q.shape[1] // LANES):
        lanes = slice(pair * LANES, (pair + 1) * LANES)
        for start in range(0, rows, block):
            count = min(block, rows - start)
            key_at = start + count - block
            keys2, vals2 = two_heads(k[key_at : key_at + block, lanes], v[key_at : key_at + block, lanes])
            scores = dot_t(q[start : start + count, lanes], keys2)
            own = (iota((count, 2 * block), 0) + (start - key_at)) // frames
            other = (iota((count, 2 * block), 1) % block) // frames
            scores = jnp.where(own == other, scores, MASKED)
            halves = [scores[:, :block], scores[:, block:]]
            halves = [jnp.exp2(part - jnp.max(part, axis=-1, keepdims=True)).astype(BF16) for part in halves]
            result = weighted(jnp.concatenate(halves, axis=1), vals2)
            out[start : start + count, at + pair * LANES : at + (pair + 1) * LANES] = result


def temporal_kernel(count, a_ref, own_ref, *refs):
    pieces = refs[:count]
    out_ref, att_ref, other_ref, sems = refs[count:]
    starts = part_starts(pieces[0].shape[1], pieces[4].shape[1])
    fetched = piece_copies(pieces, starts, other_ref, sems)
    for copy in fetched:
        copy.start()
    frames = a_ref.shape[0]
    local = own_ref.shape[-1]
    main, extra = load_packed(a_ref)
    size = main.shape[0]
    row = iota((size, size), 0)
    col = iota((size, size), 1)
    swap = jnp.where((row % frames) * ROWS + row // frames == col, 1.0, 0.0).astype(BF16)
    x = jnp.concatenate([dot(swap, main).astype(BF16), extra], axis=0)
    for member, weights in enumerate((own_ref, other_ref)):
        for copy in fetched if member else ():
            copy.wait()
        q = (dot(x, weights[0]) * SCALE).astype(BF16)
        k = dot(x, weights[1]).astype(BF16)
        v = dot(x, weights[2]).astype(BF16)
        temporal_pairs(q, k, v, att_ref, member * local, frames)
    back = jnp.where((row % ROWS) * frames + row // ROWS == col, 1.0, 0.0).astype(BF16)
    store_packed(out_ref, dot(back, att_ref[:size, :]), att_ref[size:, :])


def middle_kernel(mine, r_ref, x_ref, p_own, p_other, gain_ref, w_own, w_other, mid_ref, qkv_ref, held, sem):
    half = held.shape[0]
    copy = pltpu.make_async_copy(x_ref.at[half_rows(half, mine), :], held, sem)
    copy.start()
    main, extra = load_packed(r_ref)
    att = jnp.concatenate([main, extra], axis=0)
    local = p_own.shape[0]
    first, second = (p_own, p_other) if mine else (p_other, p_own)
    summed = dot(att[:, :local], first[...]) + dot(att[:, local:], second[...])
    copy.wait()
    mid = (held[...].astype(F32) + summed).astype(BF16)
    mid_ref[...] = mid
    normed = layer_norm(mid.astype(F32), gain_ref[...])
    for at, w_ref in enumerate((w_own, w_other)):
        lanes = slice(at * local, (at + 1) * local)
        qkv_ref[0, :, lanes] = (dot(normed, w_ref[0]) * SCALE).astype(BF16)
        qkv_ref[1, :, lanes] = dot(normed, w_ref[1]).astype(BF16)
        qkv_ref[2, :, lanes] = dot(normed, w_ref[2]).astype(BF16)


def spatial_kernel(own_ref, other_ref, mid_own, mid_other, p_own, p_other, out_ref, att_ref):
    half, width = mid_own.shape
    patches = 2 * half
    local = p_own.shape[0]
    split = patches // LANES * LANES
    low = iota((1, LANES), 1) < HD
    for pair in range(width // LANES):
        lanes = slice(pair * LANES, (pair + 1) * LANES)
        keys2, vals2 = two_heads(
            jnp.concatenate([own_ref[1, :, lanes], other_ref[1, :, lanes]], axis=0),
            jnp.concatenate([own_ref[2, :, lanes], other_ref[2, :, lanes]], axis=0),
        )
        for part, ref in enumerate((own_ref, other_ref)):
            scores = dot_t(ref[0, :, lanes], keys2)
            left = scores[:, :split]
            both = scores[:, split : split + LANES]
            right = scores[:, split + LANES :]
            top_left = jnp.maximum(
                jnp.max(left, axis=-1, keepdims=True),
                jnp.max(jnp.where(low, both, MASKED), axis=-1, keepdims=True),
            )
            top_right = jnp.maximum(
                jnp.max(right, axis=-1, keepdims=True),
                jnp.max(jnp.where(low, MASKED, both), axis=-1, keepdims=True),
            )
            moved = (left - top_left, both - jnp.where(low, top_left, top_right), right - top_right)
            weights = jnp.concatenate([jnp.exp2(value).astype(BF16) for value in moved], axis=1)
            att_ref[part * half : (part + 1) * half, lanes] = weighted(weights, vals2)
    for part, (mine, mid) in enumerate(((True, mid_own), (False, mid_other))):
        here = slice(part * half, (part + 1) * half)
        total = mid[...].astype(F32) + dot(att_ref[here, :local], p_own[...])
        total = total + dot(att_ref[here, local:], p_other[...])
        out_ref[half_rows(half, mine), :] = total.astype(BF16)


def call(kernel, out, places, scratch=(), us=0, limit=24, spots=None):
    spaces = {"a": pl.ANY, "v": pltpu.VMEM}
    many = isinstance(out, tuple)
    spots = spots or "v" * (len(out) if many else 1)
    spots = [pl.BlockSpec(memory_space=spaces[spot]) for spot in spots]
    return pl.pallas_call(
        kernel,
        out_shape=out,
        in_specs=[pl.BlockSpec(memory_space=spaces[place]) for place in places],
        out_specs=tuple(spots) if many else spots[0],
        scratch_shapes=list(scratch),
        compiler_params=pltpu.CompilerParams(vmem_limit_bytes=limit * 1024 * 1024),
        cost_estimate=pl.CostEstimate(
            flops=int(us * 1000000000), bytes_accessed=1000000, transcendentals=0
        ),
    )


def shape(*dims, dtype=BF16):
    return jax.ShapeDtypeStruct(dims, dtype)


def routes():
    devices = [(y, c, m) for y in (0, 1) for c in (0, 1) for m in (0, 1)]

    def index(y, c, m):
        return y * 4 + c * 2 + m

    across = [(index(y, c, m), index(1 - y, c, 1 - m)) for y, c, m in devices]
    beside = [(index(y, c, m), index(1 - y, c, m)) for y, c, m in devices]
    core = [(index(y, c, m), index(y, 1 - c, m)) for y, c, m in devices]
    return across, beside, core


def fetch(piece):
    return lax.ppermute(piece, ("clip", "mp"), routes()[0])


def to_beside(piece):
    return lax.ppermute(piece, ("clip", "mp"), routes()[1])


def to_core(piece):
    return lax.ppermute(piece, ("clip", "mp"), routes()[2])


def share_parts(first, second):
    chip = to_beside(first)
    return [first, to_core(first), chip, to_core(chip), second, to_core(second)]


def all_to_all(values):
    return lax.all_to_all(values, "tm", split_axis=0, concat_axis=0, tiled=True)


def in_hbm(value):
    return pltpu.with_memory_space_constraint(value, pltpu.HBM)


def in_vmem(value):
    return pltpu.with_memory_space_constraint(value, pltpu.VMEM)


def shards(video, gain_time, qkv_time, proj_time, gain_space, qkv_space, proj_space):
    _, patches, width = video.shape
    frames = lax.axis_size("tm")
    local = qkv_time.shape[-1]
    half = patches // 2
    x = video[0]
    w_time = jnp.transpose(qkv_time, (1, 0, 2))
    w_space = jnp.transpose(qkv_space, (1, 0, 2))
    gain_time = gain_time.reshape(1, width)
    gain_space = gain_space.reshape(1, width)
    packed = shape(frames, ROWS, width + LANES)
    dma = pltpu.SemaphoreType.DMA

    rows = width // 64 * 10
    rest = width // 2 - 2 * rows
    first = fetch(call(cut_kernel, shape(3, rows, local), "a", [dma])(in_hbm(w_time)))
    sent, second = call(
        norm_kernel,
        (packed, shape(3, rest, local)),
        "aaa",
        [pltpu.VMEM((half, width), BF16), pltpu.VMEM((1, width), F32), dma((3,))],
    )(in_hbm(x), in_hbm(gain_time), in_hbm(w_time))
    first, w_space_, proj_time_, proj_space_ = lax.optimization_barrier((first, w_space, proj_time, proj_space))
    second, w_late = lax.optimization_barrier((fetch(second), w_space_))
    pieces = share_parts(first, second)
    arrived = all_to_all(sent)
    held = pltpu.VMEM(w_time.shape, BF16)
    attended = call(
        functools.partial(temporal_kernel, len(pieces)),
        packed,
        "vv" + "a" * len(pieces),
        [pltpu.VMEM((half, width), BF16), held, dma((len(pieces),))],
    )(arrived, w_time, *[in_hbm(p) for p in pieces])
    back = all_to_all(attended)

    quarter = local // 4
    rows = width // 64 * 6
    rest = width // 2 - 2 * rows
    height = 3 * rows + 4 * quarter
    mixed = call(functools.partial(cut_more_kernel, rows), shape(height, local), "aaa", [dma((7,))])(
        in_hbm(w_space_), in_hbm(proj_time_), in_hbm(proj_space_)
    )
    far = call(cut_rest_kernel, shape(3, rest, local), "a", [dma])(in_hbm(w_late))
    mixed, _ = lax.optimization_barrier((fetch(mixed), attended))
    more = share_parts(mixed, fetch(far))
    space_other, other_time, other_space = call(
        join_kernel,
        (pltpu.VMEM(w_space.shape, BF16), shape(local, width), shape(local, width)),
        "aaaaaa",
        [dma((30,))],
        us=C_JOIN,
    )(*more)

    theirs = lax.ppermute(back, "mp", [(0, 1), (1, 0)])
    made = []
    for mine, values in ((True, back), (False, theirs)):
        made.append(
            call(
                functools.partial(middle_kernel, mine),
                (shape(half, width), shape(3, half, width)),
                "vavvvvv",
                [pltpu.VMEM((half, width), BF16), dma],
            )(values, x, proj_time, other_time, gain_space, w_space, in_vmem(space_other))
        )
    (mid_own, qkv_own), (mid_other, qkv_other) = made
    out = call(spatial_kernel, shape(patches, width), "vvvvvv", [pltpu.VMEM((patches, width), BF16)])(
        qkv_own, qkv_other, mid_own, mid_other, proj_space, other_space
    )
    return out[None]


def solution(mesh):
    placed = (
        P(("clip", "tm"), None, None),
        P(),
        P(None, None, "mp"),
        P("mp", None),
        P(),
        P(None, None, "mp"),
        P("mp", None),
    )
    return jax.shard_map(
        shards, mesh=mesh, in_specs=placed, out_specs=P(("clip", "tm"), None, None), check_vma=False
    )
```

time: 117 us -> 106 us (0.906); the launches traced: 115 us -> 105 us
  starting transfers between devices: 50.1 us -> 39.7 us
  Pallas kernels: 30 us -> 35 us
  waiting for transfers between devices: 32.3 us -> 28.3 us
    ppermute x4 -> x0, starting transfers between devices: 6.51 us -> none  [shards(): partner.append(lax.ppermute(part, 'mp', [(0, 1), (1, 0)]))]
    ppermute x7 -> x6, starting transfers between devices: 15.8 us -> 9.39 us  [to_core(): return lax.ppermute(piece, ('clip', 'mp'), routes()[2])]
    ppermute x3 -> x2, waiting for transfers between devices: 0.34 us -> 5.78 us  [to_beside(): return lax.ppermute(piece, ('clip', 'mp'), routes()[1])]
    ppermute x4, waiting for transfers between devices: 19 us -> 15.1 us  [fetch(): return lax.ppermute(piece, ('clip', 'mp'), routes()[0])]
    ppermute x1, waiting for transfers between devices: 9.2 us -> 5.51 us  [shards(): theirs = lax.ppermute(back, 'mp', [(0, 1), (1, 0)])]
    pallas_call x2, Pallas kernels: 4.98 us -> 7.79 us  [shards(): call(functools.partial(middle_kernel, mine), (shape(half, width), shape(3...]
    ppermute x4, starting transfers between devices: 6.53 us -> 8.97 us  [fetch(): return lax.ppermute(piece, ('clip', 'mp'), routes()[0])]
    ppermute x4 -> x0, waiting for transfers between devices: 2.42 us -> none  [shards(): partner.append(lax.ppermute(part, 'mp', [(0, 1), (1, 0)]))]
  transfers between devices with their start and end apart: 21 -> 15, of which waited for: 8 -> 5; matrix products, arithmetic and copies ran while one was open for 0% -> 0% of each run, Pallas kernels for 16% -> 19%
where the time goes in v3:
time: 106 us; the launch traced here: 105 us
  starting transfers between devices  39.7 us (37%)
  Pallas kernels  35 us (33%)
  waiting for transfers between devices  28.3 us (27%)
  local copies, waits for them, and re-layouts  2.06 us (2%)
    all_to_all x2, starting transfers between devices, all_to_all(): return lax.all_to_all(values, 'tm', split_axis=0, concat_axis=0, tiled=True)  20.8 us
    ppermute x4, waiting for transfers between devices, fetch(): return lax.ppermute(piece, ('clip', 'mp'), routes()[0])  15.1 us
    pallas_call x1, Pallas kernels, shards(): call(spatial_kernel, shape(patches, width), 'vvvvvv', [pltpu.VMEM((patche...  10.1 us
    ppermute x6, starting transfers between devices, to_core(): return lax.ppermute(piece, ('clip', 'mp'), routes()[2])  9.39 us
    ppermute x4, starting transfers between devices, fetch(): return lax.ppermute(piece, ('clip', 'mp'), routes()[0])  8.97 us
    pallas_call x2, Pallas kernels, shards(): call(functools.partial(middle_kernel, mine), (shape(half, width), shape(3...  7.79 us
    pallas_call x1, Pallas kernels, shards(): call(functools.partial(temporal_kernel, len(pieces)), packed, 'vv' + 'a'...  6.16 us
    ppermute x2, waiting for transfers between devices, to_beside(): return lax.ppermute(piece, ('clip', 'mp'), routes()[1])  5.78 us
  transfers between devices with their start and end apart: 15, of which 5 were waited for; matrix products, arithmetic and copies ran while one was open for 0% of the time, Pallas kernels for 19%

profile of v3, /device:TPU:1, one launch (start us, length us, event | category | flops | bytes accessed | tf_op | source)
XLA Modules:
  0.0 105.3 jit_solution(12055776324448355690)
XLA Ops:
  0.0 1.0 shard_map.74
  1.0 3.7 %collective-permute-start = (bf16[3,160,512]{2,1,0:T(8,128)(2,1)S(1)}, bf16[3,160,512]{2,1,0:T(8,128)(2,1)}, u32[]{:S(2)}, u32[]{:S(2)}) collective-permute-start(bf16[3,160,512]{2,1,0:T(8,128)(2,1)S(1)} %shard_map.74), channel_id=1, source_target_pairs={{0,129},{1,128},{64,193},{65,192},{128,1},{129,0},{192,65},{193,64... | collective-permute-start | bytes 1474568 | tf_op jit(solution)/shard_map/ppermute | solution.py:339
  4.7 2.7 %shard_map.73 = (bf16[32,8,1152]{2,1,0:T(8,128)(2,1)}, bf16[3,192,512]{2,1,0:T(8,128)(2,1)}) custom-call(bf16[576,1024]{1,0:T(8,128)(2,1)} %bitcast.13, f32[1,1024]{1,0:T(1,128)} %bitcast.18, bf16[3,1024,512]{2,1,0:T(8,128)(2,1)} %bitcast.11), custom_call_target="tpu_custom_call" | custom-call | bytes 1000000 | tf_op jit(solution)/shard_map/pallas_call | solution.py:383
  7.4 0.1 collective-permute-start.4
  7.5 11.1 %all-to-all-start = ((bf16[32,8,1152]{2,1,0:T(8,128)(2,1)}), bf16[32,8,1152]{2,1,0:T(8,128)(2,1)}, u32[]{:S(2)}, u32[]{:S(2)}) async-start(bf16[32,8,1152]{2,1,0:T(8,128)(2,1)} %get-tuple-element.21), calls=%async_computation | async-start | bytes 1179648 | tf_op jit(solution)/shard_map/all_to_all | solution.py:356
  18.7 0.1 collective-permute-start.2
  18.8 2.2 %shard_map.76 = bf16[800,512]{1,0:T(8,128)(2,1)} custom-call(bf16[3,1024,512]{2,1,0:T(8,128)(2,1)} %bitcast.6, bf16[512,1024]{1,0:T(8,128)(2,1)} %p_own.4, bf16[512,1024]{1,0:T(8,128)(2,1)} %p_own.5), custom_call_target="tpu_custom_call" | custom-call | bytes 1000000 | tf_op jit(solution)/shard_map/pallas_call | solution.py:406
  21.0 2.7 %collective-permute-start.6 = (bf16[800,512]{1,0:T(8,128)(2,1)}, bf16[800,512]{1,0:T(8,128)(2,1)}, u32[]{:S(2)}, u32[]{:S(2)}) collective-permute-start(bf16[800,512]{1,0:T(8,128)(2,1)} %shard_map.76), channel_id=1, source_target_pairs={{0,129},{1,128},{64,193},{65,192},{128,1},{129,0},{192,65},{193,64... | collective-permute-start | bytes 2457608 | tf_op jit(solution)/shard_map/ppermute | solution.py:339
  23.7 3.6 %collective-permute-done.4.refs_4_ = bf16[3,192,512]{2,1,0:T(8,128)(2,1)} collective-permute-done((bf16[3,192,512]{2,1,0:T(8,128)(2,1)}, bf16[3,192,512]{2,1,0:T(8,128)(2,1)}, u32[]{:S(2)}, u32[]{:S(2)}) %collective-permute-start.4) | collective-permute-done | bytes 589856 | tf_op jit(solution)/shard_map/ppermute | solution.py:339
  27.3 5.2 %collective-permute-start.5 = (bf16[3,192,512]{2,1,0:T(8,128)(2,1)}, bf16[3,192,512]{2,1,0:T(8,128)(2,1)}, u32[]{:S(2)}, u32[]{:S(2)}) collective-permute-start(bf16[3,192,512]{2,1,0:T(8,128)(2,1)} %collective-permute-done.4.refs_4_), channel_id=1, source_target_pairs={{0,64},{1,65},{64,0},{65,1},{128,192},{129,193},{192,128},{193,129... | collective-permute-start | bytes 1769480 | tf_op jit(solution)/shard_map/ppermute | solution.py:347
  32.5 0.5 collective-permute-start.3
  33.0 2.2 %shard_map.77 = bf16[3,320,512]{2,1,0:T(8,128)(2,1)} custom-call(bf16[3,1024,512]{2,1,0:T(8,128)(2,1)} %bitcast.7), custom_call_target="tpu_custom_call" | custom-call | bytes 1000000 | tf_op jit(solution)/shard_map/pallas_call | solution.py:409
  35.2 2.5 %collective-permute-start.10 = (bf16[3,320,512]{2,1,0:T(8,128)(2,1)}, bf16[3,320,512]{2,1,0:T(8,128)(2,1)}, u32[]{:S(2)}, u32[]{:S(2)}) collective-permute-start(bf16[3,320,512]{2,1,0:T(8,128)(2,1)} %shard_map.77), channel_id=1, source_target_pairs={{0,129},{1,128},{64,193},{65,192},{128,1},{129,0},{192,65},{193,64... | collective-permute-start | bytes 2949128 | tf_op jit(solution)/shard_map/ppermute | solution.py:339
  37.7 6.2 %shard_map.75 = bf16[32,8,1152]{2,1,0:T(8,128)(2,1)S(1)} custom-call(bf16[32,8,1152]{2,1,0:T(8,128)(2,1)} %all-to-all-done.a_ref, bf16[3,1024,512]{2,1,0:T(8,128)(2,1)S(1)} %bitcast.12, bf16[3,160,512]{2,1,0:T(8,128)(2,1)} %collective-permute-done.refs_0_, bf16[3,160,512]{2,1,0:T(8,128)(2,1)} %collective-permute-done.1.refs_1_, ...), custom_call_target="tpu_custom_call" | custom-call | bytes 1000000 | tf_op jit(solution)/shard_map/pallas_call | solution.py:394
  43.8 0.8 copy-done.5
  44.7 9.7 %all-to-all-start.1 = ((bf16[32,8,1152]{2,1,0:T(8,128)(2,1)}), bf16[32,8,1152]{2,1,0:T(8,128)(2,1)}, u32[]{:S(2)}, u32[]{:S(2)}) async-start(bf16[32,8,1152]{2,1,0:T(8,128)(2,1)} %copy-done.5), calls=%async_computation.1 | async-start | bytes 1179648 | tf_op jit(solution)/shard_map/all_to_all | solution.py:356
  54.4 0.0 copy-start
  54.4 0.0 copy-start.6
  54.4 0.1 collective-permute-start.8
  54.5 11.5 %collective-permute-done.10.rest_ref = bf16[3,320,512]{2,1,0:T(8,128)(2,1)} collective-permute-done((bf16[3,320,512]{2,1,0:T(8,128)(2,1)}, bf16[3,320,512]{2,1,0:T(8,128)(2,1)}, u32[]{:S(2)}, u32[]{:S(2)}) %collective-permute-start.10) | collective-permute-done | bytes 983072 | tf_op jit(solution)/shard_map/ppermute | solution.py:339
  66.0 2.3 %collective-permute-start.11 = (bf16[3,320,512]{2,1,0:T(8,128)(2,1)}, bf16[3,320,512]{2,1,0:T(8,128)(2,1)}, u32[]{:S(2)}, u32[]{:S(2)}) collective-permute-start(bf16[3,320,512]{2,1,0:T(8,128)(2,1)} %collective-permute-done.10.rest_ref), channel_id=1, source_target_pairs={{0,64},{1,65},{64,0},{65,1},{128,192},{129,193},{192,128},{193,129... | collective-permute-start | bytes 2949128 | tf_op jit(solution)/shard_map/ppermute | solution.py:347
  68.2 5.8 %collective-permute-done.8.third_ref = bf16[800,512]{1,0:T(8,128)(2,1)} collective-permute-done((bf16[800,512]{1,0:T(8,128)(2,1)}, bf16[800,512]{1,0:T(8,128)(2,1)}, u32[]{:S(2)}, u32[]{:S(2)}) %collective-permute-start.8) | collective-permute-done | bytes 819232 | tf_op jit(solution)/shard_map/ppermute | solution.py:343
  74.0 1.4 %collective-permute-start.9 = (bf16[800,512]{1,0:T(8,128)(2,1)}, bf16[800,512]{1,0:T(8,128)(2,1)}, u32[]{:S(2)}, u32[]{:S(2)}) collective-permute-start(bf16[800,512]{1,0:T(8,128)(2,1)} %collective-permute-done.8.third_ref), channel_id=1, source_target_pairs={{0,64},{1,65},{64,0},{65,1},{128,192},{129,193},{192,128},{193,129... | collective-permute-start | bytes 2457608 | tf_op jit(solution)/shard_map/ppermute | solution.py:347
  75.5 0.3 collective-permute-start.12
  75.8 2.0 %collective-permute-done.9.fourth_ref = bf16[800,512]{1,0:T(8,128)(2,1)} collective-permute-done((bf16[800,512]{1,0:T(8,128)(2,1)}, bf16[800,512]{1,0:T(8,128)(2,1)}, u32[]{:S(2)}, u32[]{:S(2)}) %collective-permute-start.9) | collective-permute-done | bytes 819232 | tf_op jit(solution)/shard_map/ppermute | solution.py:347
  77.8 2.9 %shard_map.78 = (bf16[3,1024,512]{2,1,0:T(8,128)(2,1)S(1)}, bf16[512,1024]{1,0:T(8,128)(2,1)S(1)}, bf16[512,1024]{1,0:T(8,128)(2,1)S(1)}) custom-call(bf16[800,512]{1,0:T(8,128)(2,1)} %collective-permute-done.6.first_ref, bf16[800,512]{1,0:T(8,128)(2,1)} %collective-permute-done.7.second_ref, bf16[800,512]{1,0:T(8,128)(2,1)} %collective-permute-done.8.third_ref, ...), custom_call_target="tpu_custom_call" | custom-call | flops 1000000000 | bytes 1000000 | tf_op jit(solution)/shard_map/pallas_call | solution.py:412
  80.7 0.0 copy-start.3
  80.7 1.2 %copy-done.3 = bf16[512,1024]{1,0:T(8,128)(2,1)S(1)} copy-done((bf16[512,1024]{1,0:T(8,128)(2,1)S(1)}, bf16[512,1024]{1,0:T(8,128)(2,1)}, u32[]{:S(2)}) %copy-start.3) | copy-done | bytes 1048600
  81.9 4.4 %shard_map.79 = (bf16[288,1024]{1,0:T(8,128)(2,1)S(1)}, bf16[3,288,1024]{2,1,0:T(8,128)(2,1)S(1)}) custom-call(bf16[32,8,1152]{2,1,0:T(8,128)(2,1)} %all-to-all-done.1.r_ref, bf16[576,1024]{1,0:T(8,128)(2,1)S(1)} %bitcast.14, bf16[512,1024]{1,0:T(8,128)(2,1)S(1)} %copy-done.3, bf16[512,1024]{1,0:T(8,128)(2,1)S(1)} %get-tuple-element.30.p_other, ...), custom_call_target="tpu_custom_call" | custom-call | bytes 1000000 | tf_op jit(solution)/shard_map/pallas_call | solution.py:424
  86.3 5.5 %collective-permute-done.12.r_ref = bf16[32,8,1152]{2,1,0:T(8,128)(2,1)S(1)} collective-permute-done((bf16[32,8,1152]{2,1,0:T(8,128)(2,1)}, bf16[32,8,1152]{2,1,0:T(8,128)(2,1)S(1)}, u32[]{:S(2)}, u32[]{:S(2)}) %collective-permute-start.12) | collective-permute-done | bytes 589856 | tf_op jit(solution)/shard_map/ppermute | solution.py:420
  91.8 3.4 %shard_map.80 = (bf16[288,1024]{1,0:T(8,128)(2,1)S(1)}, bf16[3,288,1024]{2,1,0:T(8,128)(2,1)S(1)}) custom-call(bf16[32,8,1152]{2,1,0:T(8,128)(2,1)S(1)} %collective-permute-done.12.r_ref, bf16[576,1024]{1,0:T(8,128)(2,1)S(1)} %bitcast.15, bf16[512,1024]{1,0:T(8,128)(2,1)S(1)} %copy-done.3, bf16[512,1024]{1,0:T(8,128)(2,1)S(1)} %get-tuple-element.30.p_other, ...), custom_call_target="tpu_custom_call" | custom-call | bytes 1000000 | tf_op jit(solution)/shard_map/pallas_call | solution.py:424
  95.2 10.1 %shard_map.81 = bf16[576,1024]{1,0:T(8,128)(2,1)} custom-call(bf16[3,288,1024]{2,1,0:T(8,128)(2,1)S(1)} %get-tuple-element.32.own_ref, bf16[3,288,1024]{2,1,0:T(8,128)(2,1)S(1)} %get-tuple-element.33.other_ref, bf16[288,1024]{1,0:T(8,128)(2,1)S(1)} %get-tuple-element.34.mid_own, bf16[288,1024]{1,0:T(8,128)(2,1)S(1)} %get-tuple-element.35.mid_other, ...), custom_call_target="tpu_custom_call" | custom-call | bytes 1000000 | tf_op jit(solution)/shard_map/pallas_call | solution.py:432
  (21 shorter events, 0.1 us)
Async XLA Ops:
  1.0 17.6 %collective-permute-start = (bf16[3,160,512]{2,1,0:T(8,128)(2,1)S(1)}, bf16[3,160,512]{2,1,0:T(8,128)(2,1)}, u32[]{:S(2)}, u32[]{:S(2)}) collective-permute-start(bf16[3,160,512]{2,1,0:T(8,128)(2,1)S(1)} %shard_map.74), channel_id=1, source_target_pairs={{0,129},{1,128},{64,193},{65,192},{128,1},{129,0},{192,65},{193,64... | collective-permute-start | bytes 1474568 | tf_op jit(solution)/shard_map/ppermute | solution.py:339
  7.4 19.9 %collective-permute-start.4 = (bf16[3,192,512]{2,1,0:T(8,128)(2,1)}, bf16[3,192,512]{2,1,0:T(8,128)(2,1)}, u32[]{:S(2)}, u32[]{:S(2)}) collective-permute-start(bf16[3,192,512]{2,1,0:T(8,128)(2,1)} %get-tuple-element.23), channel_id=1, source_target_pairs={{0,129},{1,128},{64,193},{65,192},{128,1},{129,0},{192,65},{193,64... | collective-permute-start | bytes 1769480 | tf_op jit(solution)/shard_map/ppermute | solution.py:339
  7.5 30.1 %all-to-all-start = ((bf16[32,8,1152]{2,1,0:T(8,128)(2,1)}), bf16[32,8,1152]{2,1,0:T(8,128)(2,1)}, u32[]{:S(2)}, u32[]{:S(2)}) async-start(bf16[32,8,1152]{2,1,0:T(8,128)(2,1)} %get-tuple-element.21), calls=%async_computation | async-start | bytes 1179648 | tf_op jit(solution)/shard_map/all_to_all | solution.py:356
  18.7 13.8 %collective-permute-start.2 = (bf16[3,160,512]{2,1,0:T(8,128)(2,1)}, bf16[3,160,512]{2,1,0:T(8,128)(2,1)}, u32[]{:S(2)}, u32[]{:S(2)}) collective-permute-start(bf16[3,160,512]{2,1,0:T(8,128)(2,1)} %collective-permute-done.refs_0_), channel_id=1, source_target_pairs={{0,128},{1,129},{64,192},{65,193},{128,0},{129,1},{192,64},{193,65... | collective-permute-start | bytes 1474568 | tf_op jit(solution)/shard_map/ppermute | solution.py:343
  21.0 16.7 %copy-start.1 = (bf16[1024,3,512]{2,0,1:T(8,128)(2,1)S(1)}, bf16[1024,3,512]{2,0,1:T(8,128)(2,1)}, u32[]{:S(2)}) copy-start(bf16[1024,3,512]{2,0,1:T(8,128)(2,1)} %param.9) | copy-start | bytes 9437188
  21.0 33.4 %collective-permute-start.6 = (bf16[800,512]{1,0:T(8,128)(2,1)}, bf16[800,512]{1,0:T(8,128)(2,1)}, u32[]{:S(2)}, u32[]{:S(2)}) collective-permute-start(bf16[800,512]{1,0:T(8,128)(2,1)} %shard_map.76), channel_id=1, source_target_pairs={{0,129},{1,128},{64,193},{65,192},{128,1},{129,0},{192,65},{193,64... | collective-permute-start | bytes 2457608 | tf_op jit(solution)/shard_map/ppermute | solution.py:339
  27.3 10.3 %collective-permute-start.5 = (bf16[3,192,512]{2,1,0:T(8,128)(2,1)}, bf16[3,192,512]{2,1,0:T(8,128)(2,1)}, u32[]{:S(2)}, u32[]{:S(2)}) collective-permute-start(bf16[3,192,512]{2,1,0:T(8,128)(2,1)} %collective-permute-done.4.refs_4_), channel_id=1, source_target_pairs={{0,64},{1,65},{64,0},{65,1},{128,192},{129,193},{192,128},{193,129... | collective-permute-start | bytes 1769480 | tf_op jit(solution)/shard_map/ppermute | solution.py:347
  32.5 5.1 %collective-permute-start.1 = (bf16[3,160,512]{2,1,0:T(8,128)(2,1)}, bf16[3,160,512]{2,1,0:T(8,128)(2,1)}, u32[]{:S(2)}, u32[]{:S(2)}) collective-permute-start(bf16[3,160,512]{2,1,0:T(8,128)(2,1)} %collective-permute-done.refs_0_), channel_id=1, source_target_pairs={{0,64},{1,65},{64,0},{65,1},{128,192},{129,193},{192,128},{193,129... | collective-permute-start | bytes 1474568 | tf_op jit(solution)/shard_map/ppermute | solution.py:347
  32.5 5.2 %collective-permute-start.3 = (bf16[3,160,512]{2,1,0:T(8,128)(2,1)}, bf16[3,160,512]{2,1,0:T(8,128)(2,1)}, u32[]{:S(2)}, u32[]{:S(2)}) collective-permute-start(bf16[3,160,512]{2,1,0:T(8,128)(2,1)} %collective-permute-done.2.refs_2_), channel_id=1, source_target_pairs={{0,64},{1,65},{64,0},{65,1},{128,192},{129,193},{192,128},{193,129... | collective-permute-start | bytes 1474568 | tf_op jit(solution)/shard_map/ppermute | solution.py:347
  35.2 30.8 %collective-permute-start.10 = (bf16[3,320,512]{2,1,0:T(8,128)(2,1)}, bf16[3,320,512]{2,1,0:T(8,128)(2,1)}, u32[]{:S(2)}, u32[]{:S(2)}) collective-permute-start(bf16[3,320,512]{2,1,0:T(8,128)(2,1)} %shard_map.77), channel_id=1, source_target_pairs={{0,129},{1,128},{64,193},{65,192},{128,1},{129,0},{192,65},{193,64... | collective-permute-start | bytes 2949128 | tf_op jit(solution)/shard_map/ppermute | solution.py:339
  43.8 0.8 copy-start.5
  44.7 30.8 %all-to-all-start.1 = ((bf16[32,8,1152]{2,1,0:T(8,128)(2,1)}), bf16[32,8,1152]{2,1,0:T(8,128)(2,1)}, u32[]{:S(2)}, u32[]{:S(2)}) async-start(bf16[32,8,1152]{2,1,0:T(8,128)(2,1)} %copy-done.5), calls=%async_computation.1 | async-start | bytes 1179648 | tf_op jit(solution)/shard_map/all_to_all | solution.py:356
  54.4 26.3 %copy-start = (bf16[1024,3,512]{2,0,1:T(8,128)(2,1)S(1)}, bf16[1024,3,512]{2,0,1:T(8,128)(2,1)}, u32[]{:S(2)}) copy-start(bf16[1024,3,512]{2,0,1:T(8,128)(2,1)} %param.12) | copy-start | bytes 9437188
  54.4 26.3 %copy-start.6 = (f32[1024]{0:T(1024)S(1)}, f32[1024]{0:T(1024)}, u32[]{:S(2)}) copy-start(f32[1024]{0:T(1024)} %param.11) | copy-start | bytes 12292
  54.4 19.6 %collective-permute-start.8 = (bf16[800,512]{1,0:T(8,128)(2,1)}, bf16[800,512]{1,0:T(8,128)(2,1)}, u32[]{:S(2)}, u32[]{:S(2)}) collective-permute-start(bf16[800,512]{1,0:T(8,128)(2,1)} %collective-permute-done.6.first_ref), channel_id=1, source_target_pairs={{0,128},{1,129},{64,192},{65,193},{128,0},{129,1},{192,64},{193,65... | collective-permute-start | bytes 2457608 | tf_op jit(solution)/shard_map/ppermute | solution.py:343
  66.0 9.8 %collective-permute-start.11 = (bf16[3,320,512]{2,1,0:T(8,128)(2,1)}, bf16[3,320,512]{2,1,0:T(8,128)(2,1)}, u32[]{:S(2)}, u32[]{:S(2)}) collective-permute-start(bf16[3,320,512]{2,1,0:T(8,128)(2,1)} %collective-permute-done.10.rest_ref), channel_id=1, source_target_pairs={{0,64},{1,65},{64,0},{65,1},{128,192},{129,193},{192,128},{193,129... | collective-permute-start | bytes 2949128 | tf_op jit(solution)/shard_map/ppermute | solution.py:347
  68.2 7.5 %collective-permute-start.7 = (bf16[800,512]{1,0:T(8,128)(2,1)}, bf16[800,512]{1,0:T(8,128)(2,1)}, u32[]{:S(2)}, u32[]{:S(2)}) collective-permute-start(bf16[800,512]{1,0:T(8,128)(2,1)} %collective-permute-done.6.first_ref), channel_id=1, source_target_pairs={{0,64},{1,65},{64,0},{65,1},{128,192},{129,193},{192,128},{193,129... | collective-permute-start | bytes 2457608 | tf_op jit(solution)/shard_map/ppermute | solution.py:347
  74.0 3.7 %collective-permute-start.9 = (bf16[800,512]{1,0:T(8,128)(2,1)}, bf16[800,512]{1,0:T(8,128)(2,1)}, u32[]{:S(2)}, u32[]{:S(2)}) collective-permute-start(bf16[800,512]{1,0:T(8,128)(2,1)} %collective-permute-done.8.third_ref), channel_id=1, source_target_pairs={{0,64},{1,65},{64,0},{65,1},{128,192},{129,193},{192,128},{193,129... | collective-permute-start | bytes 2457608 | tf_op jit(solution)/shard_map/ppermute | solution.py:347
  75.5 5.2 %copy-start.2 = (bf16[1,576,1024]{2,1,0:T(8,128)(2,1)S(1)}, bf16[1,576,1024]{2,1,0:T(8,128)(2,1)}, u32[]{:S(2)}) copy-start(bf16[1,576,1024]{2,1,0:T(8,128)(2,1)} %param.7) | copy-start | bytes 3538948
  75.5 16.4 %collective-permute-start.12 = (bf16[32,8,1152]{2,1,0:T(8,128)(2,1)}, bf16[32,8,1152]{2,1,0:T(8,128)(2,1)S(1)}, u32[]{:S(2)}, u32[]{:S(2)}) collective-permute-start(bf16[32,8,1152]{2,1,0:T(8,128)(2,1)} %all-to-all-done.1.r_ref), channel_id=1, source_target_pairs={{0,1},{1,0},{2,3},{3,2},{4,5},{5,4},{6,7},{7,6},{8,9},{9,8},{10,11... | collective-permute-start | bytes 1769480 | tf_op jit(solution)/shard_map/ppermute | solution.py:420
  80.7 1.2 %copy-start.3 = (bf16[512,1024]{1,0:T(8,128)(2,1)S(1)}, bf16[512,1024]{1,0:T(8,128)(2,1)}, u32[]{:S(2)}) copy-start(bf16[512,1024]{1,0:T(8,128)(2,1)} %p_own.4) | copy-start | bytes 3145732
  86.3 8.9 %copy-start.4 = (bf16[512,1024]{1,0:T(8,128)(2,1)S(1)}, bf16[512,1024]{1,0:T(8,128)(2,1)}, u32[]{:S(2)}) copy-start(bf16[512,1024]{1,0:T(8,128)(2,1)} %p_own.5) | copy-start | bytes 3145732

commit v4 on v3

--- a/solution.py
+++ b/solution.py
@@ -16,7 +16,7 @@
 SCALE = math.log2(math.e) / math.sqrt(HD)
 EPS = 1e-05
 MASKED = -1e30
-C_JOIN = 1
+C_JOIN = 2
 
 
 def dot(left, right):
@@ -222,26 +222,36 @@
 
 def temporal_kernel(count, a_ref, own_ref, *refs):
     pieces = refs[:count]
-    out_ref, att_ref, other_ref, sems = refs[count:]
+    out_ref, held_ref, att_ref, other_ref, sems = refs[count:]
+    frames = held_ref.shape[0]
+    step = frames // 4
+    arriving = []
+    for at in range(4):
+        some = slice(at * step, (at + 1) * step)
+        arriving.append(pltpu.make_async_copy(a_ref.at[some], held_ref.at[some], sems.at[3, at]))
     starts = part_starts(pieces[0].shape[1], pieces[4].shape[1])
-    fetched = piece_copies(pieces, starts, other_ref, sems)
-    for copy in fetched:
+    fetched = []
+    for at in range(3):
+        fetched.append(piece_copies([piece.at[at] for piece in pieces], starts, other_ref.at[at], sems.at[at]))
+    for copy in arriving + fetched[0] + fetched[1] + fetched[2]:
         copy.start()
-    frames = a_ref.shape[0]
+    for copy in arriving:
+        copy.wait()
     local = own_ref.shape[-1]
-    main, extra = load_packed(a_ref)
+    main, extra = load_packed(held_ref)
     size = main.shape[0]
     row = iota((size, size), 0)
     col = iota((size, size), 1)
     swap = jnp.where((row % frames) * ROWS + row // frames == col, 1.0, 0.0).astype(BF16)
     x = jnp.concatenate([dot(swap, main).astype(BF16), extra], axis=0)
     for member, weights in enumerate((own_ref, other_ref)):
-        for copy in fetched if member else ():
-            copy.wait()
-        q = (dot(x, weights[0]) * SCALE).astype(BF16)
-        k = dot(x, weights[1]).astype(BF16)
-        v = dot(x, weights[2]).astype(BF16)
-        temporal_pairs(q, k, v, att_ref, member * local, frames)
+        made = []
+        for at in range(3):
+            for copy in fetched[at] if member else ():
+                copy.wait()
+            flat = dot(x, weights[at])
+            made.append((flat if at else flat * SCALE).astype(BF16))
+        temporal_pairs(*made, att_ref, member * local, frames)
     back = jnp.where((row % ROWS) * frames + row // ROWS == col, 1.0, 0.0).astype(BF16)
     store_packed(out_ref, dot(back, att_ref[:size, :]), att_ref[size:, :])
 
@@ -394,9 +404,9 @@
     attended = call(
         functools.partial(temporal_kernel, len(pieces)),
         packed,
-        "vv" + "a" * len(pieces),
-        [pltpu.VMEM((half, width), BF16), held, dma((len(pieces),))],
-    )(arrived, w_time, *[in_hbm(p) for p in pieces])
+        "av" + "a" * len(pieces),
+        [pltpu.VMEM(packed.shape, BF16), pltpu.VMEM((half, width), BF16), held, dma((4, len(pieces)))],
+    )(in_hbm(arrived), w_time, *[in_hbm(p) for p in pieces])
     back = all_to_all(attended)
 
     quarter = local // 4

time: 106 us -> 102 us (0.962)
  the two profiles are of different devices: /device:TPU:1 before, /device:TPU:48 now
where the time goes in v4:
time: 102 us
  waiting for transfers between devices  35.9 us (35%)
  Pallas kernels  33.7 us (33%)
  starting transfers between devices  30.9 us (30%)
  local copies, waits for them, and re-layouts  1.37 us (1%)
    all_to_all x2, starting transfers between devices, all_to_all(): return lax.all_to_all(values, 'tm', split_axis=0, concat_axis=0, tiled=True)  22.4 us
    ppermute x4, waiting for transfers between devices, fetch(): return lax.ppermute(piece, ('clip', 'mp'), routes()[0])  15.5 us
    all_to_all x2, waiting for transfers between devices, all_to_all(): return lax.all_to_all(values, 'tm', split_axis=0, concat_axis=0, tiled=True)  13.2 us
    pallas_call x1, Pallas kernels, shards(): call(spatial_kernel, shape(patches, width), 'vvvvvv', [pltpu.VMEM((patche...  10 us
    pallas_call x2, Pallas kernels, shards(): call(functools.partial(middle_kernel, mine), (shape(half, width), shape(3...  6.92 us
    pallas_call x1, Pallas kernels, shards(): call(functools.partial(temporal_kernel, len(pieces)), packed, 'av' + 'a'...  5.62 us
    ppermute x1, waiting for transfers between devices, shards(): theirs = lax.ppermute(back, 'mp', [(0, 1), (1, 0)])  5.48 us
    ppermute x2, starting transfers between devices, to_beside(): return lax.ppermute(piece, ('clip', 'mp'), routes()[1])  5.08 us
  transfers between devices with their start and end apart: 15, of which 7 were waited for; matrix products, arithmetic and copies ran while one was open for 0% of the time, Pallas kernels for 19%

profile of v4, /device:TPU:48, one launch (start us, length us, event | category | flops | bytes accessed | tf_op | source)
XLA Modules:
  0.0 102.1 jit_solution(13595001639865898836)
XLA Ops:
  0.0 1.0 %shard_map.74 = bf16[3,160,512]{2,1,0:T(8,128)(2,1)S(1)} custom-call(bf16[3,1024,512]{2,1,0:T(8,128)(2,1)} %bitcast.10), custom_call_target="tpu_custom_call" | custom-call | bytes 1000000 | tf_op jit(solution)/shard_map/pallas_call | solution.py:392
  1.0 0.5 collective-permute-start
  1.6 2.7 %shard_map.73 = (bf16[32,8,1152]{2,1,0:T(8,128)(2,1)}, bf16[3,192,512]{2,1,0:T(8,128)(2,1)}) custom-call(bf16[576,1024]{1,0:T(8,128)(2,1)} %bitcast.13, f32[1,1024]{1,0:T(1,128)} %bitcast.18, bf16[3,1024,512]{2,1,0:T(8,128)(2,1)} %bitcast.11), custom_call_target="tpu_custom_call" | custom-call | bytes 1000000 | tf_op jit(solution)/shard_map/pallas_call | solution.py:393
  4.3 1.7 %collective-permute-start.4 = (bf16[3,192,512]{2,1,0:T(8,128)(2,1)}, bf16[3,192,512]{2,1,0:T(8,128)(2,1)}, u32[]{:S(2)}, u32[]{:S(2)}) collective-permute-start(bf16[3,192,512]{2,1,0:T(8,128)(2,1)} %get-tuple-element.23), channel_id=1, source_target_pairs={{0,129},{1,128},{64,193},{65,192},{128,1},{129,0},{192,65},{193,64... | collective-permute-start | bytes 1769480 | tf_op jit(solution)/shard_map/ppermute | solution.py:349
  6.0 11.2 %all-to-all-start = ((bf16[32,8,1152]{2,1,0:T(8,128)(2,1)}), bf16[32,8,1152]{2,1,0:T(8,128)(2,1)}, u32[]{:S(2)}, u32[]{:S(2)}) async-start(bf16[32,8,1152]{2,1,0:T(8,128)(2,1)} %get-tuple-element.21), calls=%async_computation | async-start | bytes 1179648 | tf_op jit(solution)/shard_map/all_to_all | solution.py:366
  17.2 2.6 %collective-permute-start.2 = (bf16[3,160,512]{2,1,0:T(8,128)(2,1)}, bf16[3,160,512]{2,1,0:T(8,128)(2,1)}, u32[]{:S(2)}, u32[]{:S(2)}) collective-permute-start(bf16[3,160,512]{2,1,0:T(8,128)(2,1)} %collective-permute-done.refs_0_), channel_id=1, source_target_pairs={{0,128},{1,129},{64,192},{65,193},{128,0},{129,1},{192,64},{193,65... | collective-permute-start | bytes 1474568 | tf_op jit(solution)/shard_map/ppermute | solution.py:353
  19.8 2.2 %shard_map.76 = bf16[800,512]{1,0:T(8,128)(2,1)} custom-call(bf16[3,1024,512]{2,1,0:T(8,128)(2,1)} %bitcast.6, bf16[512,1024]{1,0:T(8,128)(2,1)} %p_own.4, bf16[512,1024]{1,0:T(8,128)(2,1)} %p_own.5), custom_call_target="tpu_custom_call" | custom-call | bytes 1000000 | tf_op jit(solution)/shard_map/pallas_call | solution.py:416
  22.0 0.0 copy-start.1
  22.0 0.1 collective-permute-start.6
  22.1 5.9 %collective-permute-done.4.refs_4_ = bf16[3,192,512]{2,1,0:T(8,128)(2,1)} collective-permute-done((bf16[3,192,512]{2,1,0:T(8,128)(2,1)}, bf16[3,192,512]{2,1,0:T(8,128)(2,1)}, u32[]{:S(2)}, u32[]{:S(2)}) %collective-permute-start.4) | collective-permute-done | bytes 589856 | tf_op jit(solution)/shard_map/ppermute | solution.py:349
  28.0 0.5 collective-permute-start.1
  28.5 1.7 %collective-permute-done.2.refs_2_ = bf16[3,160,512]{2,1,0:T(8,128)(2,1)} collective-permute-done((bf16[3,160,512]{2,1,0:T(8,128)(2,1)}, bf16[3,160,512]{2,1,0:T(8,128)(2,1)}, u32[]{:S(2)}, u32[]{:S(2)}) %collective-permute-start.2) | collective-permute-done | bytes 491552 | tf_op jit(solution)/shard_map/ppermute | solution.py:353
  30.2 2.2 %shard_map.77 = bf16[3,320,512]{2,1,0:T(8,128)(2,1)} custom-call(bf16[3,1024,512]{2,1,0:T(8,128)(2,1)} %bitcast.7), custom_call_target="tpu_custom_call" | custom-call | bytes 1000000 | tf_op jit(solution)/shard_map/pallas_call | solution.py:419
  32.4 0.1 collective-permute-start.10
  32.5 3.2 %all-to-all-done.a_ref = bf16[32,8,1152]{2,1,0:T(8,128)(2,1)} async-done(((bf16[32,8,1152]{2,1,0:T(8,128)(2,1)}), bf16[32,8,1152]{2,1,0:T(8,128)(2,1)}, u32[]{:S(2)}, u32[]{:S(2)}) %all-to-all-start) | async-done | bytes 589856 | tf_op jit(solution)/shard_map/all_to_all | solution.py:366
  35.7 5.6 %shard_map.75 = bf16[32,8,1152]{2,1,0:T(8,128)(2,1)S(1)} custom-call(bf16[32,8,1152]{2,1,0:T(8,128)(2,1)} %all-to-all-done.a_ref, bf16[3,1024,512]{2,1,0:T(8,128)(2,1)S(1)} %bitcast.12, bf16[3,160,512]{2,1,0:T(8,128)(2,1)} %collective-permute-done.refs_0_, bf16[3,160,512]{2,1,0:T(8,128)(2,1)} %collective-permute-done.1.refs_1_, ...), custom_call_target="tpu_custom_call" | custom-call | bytes 1000000 | tf_op jit(solution)/shard_map/pallas_call | solution.py:404
  41.3 0.8 copy-done.5
  42.1 3.4 %collective-permute-done.6.first_ref = bf16[800,512]{1,0:T(8,128)(2,1)} collective-permute-done((bf16[800,512]{1,0:T(8,128)(2,1)}, bf16[800,512]{1,0:T(8,128)(2,1)}, u32[]{:S(2)}, u32[]{:S(2)}) %collective-permute-start.6) | collective-permute-done | bytes 819232 | tf_op jit(solution)/shard_map/ppermute | solution.py:349
  45.5 2.5 %collective-permute-start.8 = (bf16[800,512]{1,0:T(8,128)(2,1)}, bf16[800,512]{1,0:T(8,128)(2,1)}, u32[]{:S(2)}, u32[]{:S(2)}) collective-permute-start(bf16[800,512]{1,0:T(8,128)(2,1)} %collective-permute-done.6.first_ref), channel_id=1, source_target_pairs={{0,128},{1,129},{64,192},{65,193},{128,0},{129,1},{192,64},{193,65... | collective-permute-start | bytes 2457608 | tf_op jit(solution)/shard_map/ppermute | solution.py:353
  48.0 11.2 %all-to-all-start.1 = ((bf16[32,8,1152]{2,1,0:T(8,128)(2,1)}), bf16[32,8,1152]{2,1,0:T(8,128)(2,1)S(1)}, u32[]{:S(2)}, u32[]{:S(2)}) async-start(bf16[32,8,1152]{2,1,0:T(8,128)(2,1)} %copy-done.5), calls=%async_computation.1 | async-start | bytes 1179648 | tf_op jit(solution)/shard_map/all_to_all | solution.py:366
  59.2 0.0 copy-start.3
  59.3 0.0 copy-start.6
  59.3 6.2 %collective-permute-done.10.rest_ref = bf16[3,320,512]{2,1,0:T(8,128)(2,1)} collective-permute-done((bf16[3,320,512]{2,1,0:T(8,128)(2,1)}, bf16[3,320,512]{2,1,0:T(8,128)(2,1)}, u32[]{:S(2)}, u32[]{:S(2)}) %collective-permute-start.10) | collective-permute-done | bytes 983072 | tf_op jit(solution)/shard_map/ppermute | solution.py:349
  65.5 0.5 collective-permute-start.7
  66.0 10.0 %all-to-all-done.1.r_ref = bf16[32,8,1152]{2,1,0:T(8,128)(2,1)S(1)} async-done(((bf16[32,8,1152]{2,1,0:T(8,128)(2,1)}), bf16[32,8,1152]{2,1,0:T(8,128)(2,1)S(1)}, u32[]{:S(2)}, u32[]{:S(2)}) %all-to-all-start.1) | async-done | bytes 589856 | tf_op jit(solution)/shard_map/all_to_all | solution.py:366
  76.0 0.0 copy-start
  76.0 3.0 %shard_map.78 = (bf16[3,1024,512]{2,1,0:T(8,128)(2,1)S(1)}, bf16[512,1024]{1,0:T(8,128)(2,1)S(1)}, bf16[512,1024]{1,0:T(8,128)(2,1)S(1)}) custom-call(bf16[800,512]{1,0:T(8,128)(2,1)} %collective-permute-done.6.first_ref, bf16[800,512]{1,0:T(8,128)(2,1)} %collective-permute-done.7.second_ref, bf16[800,512]{1,0:T(8,128)(2,1)} %collective-permute-done.8.third_ref, ...), custom_call_target="tpu_custom_call" | custom-call | flops 2000000000 | bytes 1000000 | tf_op jit(solution)/shard_map/pallas_call | solution.py:422
  79.1 0.5 copy-done
  79.6 3.4 %shard_map.79 = (bf16[288,1024]{1,0:T(8,128)(2,1)S(1)}, bf16[3,288,1024]{2,1,0:T(8,128)(2,1)S(1)}) custom-call(bf16[32,8,1152]{2,1,0:T(8,128)(2,1)S(1)} %all-to-all-done.1.r_ref, bf16[576,1024]{1,0:T(8,128)(2,1)S(1)} %bitcast.14, bf16[512,1024]{1,0:T(8,128)(2,1)S(1)} %copy-done.3, bf16[512,1024]{1,0:T(8,128)(2,1)S(1)} %get-tuple-element.30.p_other, ...), custom_call_target="tpu_custom_call" | custom-call | bytes 1000000 | tf_op jit(solution)/shard_map/pallas_call | solution.py:434
  83.0 5.5 %collective-permute-done.12.r_ref = bf16[32,8,1152]{2,1,0:T(8,128)(2,1)S(1)} collective-permute-done((bf16[32,8,1152]{2,1,0:T(8,128)(2,1)S(1)}, bf16[32,8,1152]{2,1,0:T(8,128)(2,1)S(1)}, u32[]{:S(2)}, u32[]{:S(2)}) %collective-permute-start.12) | collective-permute-done | bytes 589856 | tf_op jit(solution)/shard_map/ppermute | solution.py:430
  88.4 3.6 %shard_map.80 = (bf16[288,1024]{1,0:T(8,128)(2,1)S(1)}, bf16[3,288,1024]{2,1,0:T(8,128)(2,1)S(1)}) custom-call(bf16[32,8,1152]{2,1,0:T(8,128)(2,1)S(1)} %collective-permute-done.12.r_ref, bf16[576,1024]{1,0:T(8,128)(2,1)S(1)} %bitcast.15, bf16[512,1024]{1,0:T(8,128)(2,1)S(1)} %copy-done.3, bf16[512,1024]{1,0:T(8,128)(2,1)S(1)} %get-tuple-element.30.p_other, ...), custom_call_target="tpu_custom_call" | custom-call | bytes 1000000 | tf_op jit(solution)/shard_map/pallas_call | solution.py:434
  92.0 10.0 %shard_map.81 = bf16[576,1024]{1,0:T(8,128)(2,1)} custom-call(bf16[3,288,1024]{2,1,0:T(8,128)(2,1)S(1)} %get-tuple-element.32.own_ref, bf16[3,288,1024]{2,1,0:T(8,128)(2,1)S(1)} %get-tuple-element.33.other_ref, bf16[288,1024]{1,0:T(8,128)(2,1)S(1)} %get-tuple-element.34.mid_own, bf16[288,1024]{1,0:T(8,128)(2,1)S(1)} %get-tuple-element.35.mid_other, ...), custom_call_target="tpu_custom_call" | custom-call | bytes 1000000 | tf_op jit(solution)/shard_map/pallas_call | solution.py:442
  (21 shorter events, 0.1 us)
Async XLA Ops:
  1.0 16.2 %collective-permute-start = (bf16[3,160,512]{2,1,0:T(8,128)(2,1)S(1)}, bf16[3,160,512]{2,1,0:T(8,128)(2,1)}, u32[]{:S(2)}, u32[]{:S(2)}) collective-permute-start(bf16[3,160,512]{2,1,0:T(8,128)(2,1)S(1)} %shard_map.74), channel_id=1, source_target_pairs={{0,129},{1,128},{64,193},{65,192},{128,1},{129,0},{192,65},{193,64... | collective-permute-start | bytes 1474568 | tf_op jit(solution)/shard_map/ppermute | solution.py:349
  4.3 23.7 %collective-permute-start.4 = (bf16[3,192,512]{2,1,0:T(8,128)(2,1)}, bf16[3,192,512]{2,1,0:T(8,128)(2,1)}, u32[]{:S(2)}, u32[]{:S(2)}) collective-permute-start(bf16[3,192,512]{2,1,0:T(8,128)(2,1)} %get-tuple-element.23), channel_id=1, source_target_pairs={{0,129},{1,128},{64,193},{65,192},{128,1},{129,0},{192,65},{193,64... | collective-permute-start | bytes 1769480 | tf_op jit(solution)/shard_map/ppermute | solution.py:349
  6.0 29.7 %all-to-all-start = ((bf16[32,8,1152]{2,1,0:T(8,128)(2,1)}), bf16[32,8,1152]{2,1,0:T(8,128)(2,1)}, u32[]{:S(2)}, u32[]{:S(2)}) async-start(bf16[32,8,1152]{2,1,0:T(8,128)(2,1)} %get-tuple-element.21), calls=%async_computation | async-start | bytes 1179648 | tf_op jit(solution)/shard_map/all_to_all | solution.py:366
  17.2 13.0 %collective-permute-start.2 = (bf16[3,160,512]{2,1,0:T(8,128)(2,1)}, bf16[3,160,512]{2,1,0:T(8,128)(2,1)}, u32[]{:S(2)}, u32[]{:S(2)}) collective-permute-start(bf16[3,160,512]{2,1,0:T(8,128)(2,1)} %collective-permute-done.refs_0_), channel_id=1, source_target_pairs={{0,128},{1,129},{64,192},{65,193},{128,0},{129,1},{192,64},{193,65... | collective-permute-start | bytes 1474568 | tf_op jit(solution)/shard_map/ppermute | solution.py:353
  22.0 13.7 %copy-start.1 = (bf16[1024,3,512]{2,0,1:T(8,128)(2,1)S(1)}, bf16[1024,3,512]{2,0,1:T(8,128)(2,1)}, u32[]{:S(2)}) copy-start(bf16[1024,3,512]{2,0,1:T(8,128)(2,1)} %param.9) | copy-start | bytes 9437188
  22.0 23.5 %collective-permute-start.6 = (bf16[800,512]{1,0:T(8,128)(2,1)}, bf16[800,512]{1,0:T(8,128)(2,1)}, u32[]{:S(2)}, u32[]{:S(2)}) collective-permute-start(bf16[800,512]{1,0:T(8,128)(2,1)} %shard_map.76), channel_id=1, source_target_pairs={{0,129},{1,128},{64,193},{65,192},{128,1},{129,0},{192,65},{193,64... | collective-permute-start | bytes 2457608 | tf_op jit(solution)/shard_map/ppermute | solution.py:349
  28.0 7.7 %collective-permute-start.5 = (bf16[3,192,512]{2,1,0:T(8,128)(2,1)}, bf16[3,192,512]{2,1,0:T(8,128)(2,1)}, u32[]{:S(2)}, u32[]{:S(2)}) collective-permute-start(bf16[3,192,512]{2,1,0:T(8,128)(2,1)} %collective-permute-done.4.refs_4_), channel_id=1, source_target_pairs={{0,64},{1,65},{64,0},{65,1},{128,192},{129,193},{192,128},{193,129... | collective-permute-start | bytes 1769480 | tf_op jit(solution)/shard_map/ppermute | solution.py:357
  28.0 4.5 %collective-permute-start.1 = (bf16[3,160,512]{2,1,0:T(8,128)(2,1)}, bf16[3,160,512]{2,1,0:T(8,128)(2,1)}, u32[]{:S(2)}, u32[]{:S(2)}) collective-permute-start(bf16[3,160,512]{2,1,0:T(8,128)(2,1)} %collective-permute-done.refs_0_), channel_id=1, source_target_pairs={{0,64},{1,65},{64,0},{65,1},{128,192},{129,193},{192,128},{193,129... | collective-permute-start | bytes 1474568 | tf_op jit(solution)/shard_map/ppermute | solution.py:357
  30.2 5.4 %collective-permute-start.3 = (bf16[3,160,512]{2,1,0:T(8,128)(2,1)}, bf16[3,160,512]{2,1,0:T(8,128)(2,1)}, u32[]{:S(2)}, u32[]{:S(2)}) collective-permute-start(bf16[3,160,512]{2,1,0:T(8,128)(2,1)} %collective-permute-done.2.refs_2_), channel_id=1, source_target_pairs={{0,64},{1,65},{64,0},{65,1},{128,192},{129,193},{192,128},{193,129... | collective-permute-start | bytes 1474568 | tf_op jit(solution)/shard_map/ppermute | solution.py:357
  32.4 33.1 %collective-permute-start.10 = (bf16[3,320,512]{2,1,0:T(8,128)(2,1)}, bf16[3,320,512]{2,1,0:T(8,128)(2,1)}, u32[]{:S(2)}, u32[]{:S(2)}) collective-permute-start(bf16[3,320,512]{2,1,0:T(8,128)(2,1)} %shard_map.77), channel_id=1, source_target_pairs={{0,129},{1,128},{64,193},{65,192},{128,1},{129,0},{192,65},{193,64... | collective-permute-start | bytes 2949128 | tf_op jit(solution)/shard_map/ppermute | solution.py:349
  41.3 0.8 copy-start.5
  45.5 20.4 %collective-permute-start.8 = (bf16[800,512]{1,0:T(8,128)(2,1)}, bf16[800,512]{1,0:T(8,128)(2,1)}, u32[]{:S(2)}, u32[]{:S(2)}) collective-permute-start(bf16[800,512]{1,0:T(8,128)(2,1)} %collective-permute-done.6.first_ref), channel_id=1, source_target_pairs={{0,128},{1,129},{64,192},{65,193},{128,0},{129,1},{192,64},{193,65... | collective-permute-start | bytes 2457608 | tf_op jit(solution)/shard_map/ppermute | solution.py:353
  48.0 28.0 %all-to-all-start.1 = ((bf16[32,8,1152]{2,1,0:T(8,128)(2,1)}), bf16[32,8,1152]{2,1,0:T(8,128)(2,1)S(1)}, u32[]{:S(2)}, u32[]{:S(2)}) async-start(bf16[32,8,1152]{2,1,0:T(8,128)(2,1)} %copy-done.5), calls=%async_computation.1 | async-start | bytes 1179648 | tf_op jit(solution)/shard_map/all_to_all | solution.py:366
  59.2 19.8 %copy-start.2 = (bf16[1,576,1024]{2,1,0:T(8,128)(2,1)S(1)}, bf16[1,576,1024]{2,1,0:T(8,128)(2,1)}, u32[]{:S(2)}) copy-start(bf16[1,576,1024]{2,1,0:T(8,128)(2,1)} %param.7) | copy-start | bytes 3538948
  59.2 19.8 %copy-start.3 = (bf16[512,1024]{1,0:T(8,128)(2,1)S(1)}, bf16[512,1024]{1,0:T(8,128)(2,1)}, u32[]{:S(2)}) copy-start(bf16[512,1024]{1,0:T(8,128)(2,1)} %p_own.4) | copy-start | bytes 3145732
  59.3 19.8 %copy-start.6 = (f32[1024]{0:T(1024)S(1)}, f32[1024]{0:T(1024)}, u32[]{:S(2)}) copy-start(f32[1024]{0:T(1024)} %param.11) | copy-start | bytes 12292
  65.5 10.6 %collective-permute-start.11 = (bf16[3,320,512]{2,1,0:T(8,128)(2,1)}, bf16[3,320,512]{2,1,0:T(8,128)(2,1)}, u32[]{:S(2)}, u32[]{:S(2)}) collective-permute-start(bf16[3,320,512]{2,1,0:T(8,128)(2,1)} %collective-permute-done.10.rest_ref), channel_id=1, source_target_pairs={{0,64},{1,65},{64,0},{65,1},{128,192},{129,193},{192,128},{193,129... | collective-permute-start | bytes 2949128 | tf_op jit(solution)/shard_map/ppermute | solution.py:357
  65.5 10.6 %collective-permute-start.7 = (bf16[800,512]{1,0:T(8,128)(2,1)}, bf16[800,512]{1,0:T(8,128)(2,1)}, u32[]{:S(2)}, u32[]{:S(2)}) collective-permute-start(bf16[800,512]{1,0:T(8,128)(2,1)} %collective-permute-done.6.first_ref), channel_id=1, source_target_pairs={{0,64},{1,65},{64,0},{65,1},{128,192},{129,193},{192,128},{193,129... | collective-permute-start | bytes 2457608 | tf_op jit(solution)/shard_map/ppermute | solution.py:357
  66.0 10.0 %collective-permute-start.9 = (bf16[800,512]{1,0:T(8,128)(2,1)}, bf16[800,512]{1,0:T(8,128)(2,1)}, u32[]{:S(2)}, u32[]{:S(2)}) collective-permute-start(bf16[800,512]{1,0:T(8,128)(2,1)} %collective-permute-done.8.third_ref), channel_id=1, source_target_pairs={{0,64},{1,65},{64,0},{65,1},{128,192},{129,193},{192,128},{193,129... | collective-permute-start | bytes 2457608 | tf_op jit(solution)/shard_map/ppermute | solution.py:357
  76.0 12.4 %collective-permute-start.12 = (bf16[32,8,1152]{2,1,0:T(8,128)(2,1)S(1)}, bf16[32,8,1152]{2,1,0:T(8,128)(2,1)S(1)}, u32[]{:S(2)}, u32[]{:S(2)}) collective-permute-start(bf16[32,8,1152]{2,1,0:T(8,128)(2,1)S(1)} %all-to-all-done.1.r_ref), channel_id=1, source_target_pairs={{0,1},{1,0},{2,3},{3,2},{4,5},{5,4},{6,7},{7,6},{8,9},{9,8},{10,11... | collective-permute-start | bytes 1769480 | tf_op jit(solution)/shard_map/ppermute | solution.py:430
  76.0 3.6 %copy-start = (bf16[1024,3,512]{2,0,1:T(8,128)(2,1)S(1)}, bf16[1024,3,512]{2,0,1:T(8,128)(2,1)}, u32[]{:S(2)}) copy-start(bf16[1024,3,512]{2,0,1:T(8,128)(2,1)} %param.12) | copy-start | bytes 9437188
  82.9 9.1 %copy-start.4 = (bf16[512,1024]{1,0:T(8,128)(2,1)S(1)}, bf16[512,1024]{1,0:T(8,128)(2,1)}, u32[]{:S(2)}) copy-start(bf16[512,1024]{1,0:T(8,128)(2,1)} %p_own.5) | copy-start | bytes 3145732
